TPU v7x, 128 devices: a whole 4x4x4 slice. The times are simulated.
128 devices in a mesh: dp: 32 (over y, x, core), mp: 4 (over z).
Axes of the slice: x: 4, y: 4, z: 4, core: 2. Of those that a mesh axis runs over, the one named last changes fastest.
Arguments:
- tokens: bfloat16 [65536, 768], P('dp'), may hold values from -6 to 6
- time_emb: bfloat16 [512, 768], P('dp'), may hold values from -3 to 3
- segments: int32 [512, 128], P('dp'), may hold values from 0 to 3, never falling along the last dimension, each value on 1 to 64 neighbouring positions
- cotangent: bfloat16 [65536, 768], P('dp')
- w_qkv: float32 [3, 768, 768], P(None, 'dp', 'mp'), may hold values from -0.21875 to 0.21875
- w_out: float32 [768, 768], P('mp', 'dp')
- w_up: float32 [768, 3072], P('dp', 'mp'), may hold values from -0.21875 to 0.21875
- w_down: float32 [3072, 768], P('mp', 'dp')
- norm_params: float32 [4, 768], P(None, 'dp')
- qkv_first: float32 [3, 768, 768], P(None, 'dp', 'mp')
- qkv_second: float32 [3, 768, 768], P(None, 'dp', 'mp')
- out_first: float32 [768, 768], P('mp', 'dp')
- out_second: float32 [768, 768], P('mp', 'dp')
- up_first: float32 [768, 3072], P('dp', 'mp')
- up_second: float32 [768, 3072], P('dp', 'mp')
- down_first: float32 [3072, 768], P('mp', 'dp')
- down_second: float32 [3072, 768], P('mp', 'dp')
- norm_first: float32 [4, 768], P(None, 'dp')
- norm_second: float32 [4, 768], P(None, 'dp')
Outputs:
- layer_out: bfloat16 [65536, 768], P('dp')
- input_grad: bfloat16 [65536, 768], P('dp')
- grad_norm: float32 [], replicated
- qkv_moment: float32 [3, 768, 768], P(None, 'dp', 'mp')
- qkv_square: float32 [3, 768, 768], P(None, 'dp', 'mp')
- qkv_weight: float32 [3, 768, 768], P(None, 'dp', 'mp')
- out_moment: float32 [768, 768], P('mp', 'dp')
- out_square: float32 [768, 768], P('mp', 'dp')
- out_weight: float32 [768, 768], P('mp', 'dp')
- up_moment: float32 [768, 3072], P('dp', 'mp')
- up_square: float32 [768, 3072], P('dp', 'mp')
- up_weight: float32 [768, 3072], P('dp', 'mp')
- down_moment: float32 [3072, 768], P('mp', 'dp')
- down_square: float32 [3072, 768], P('mp', 'dp')
- down_weight: float32 [3072, 768], P('mp', 'dp')
- norm_moment: float32 [4, 768], P(None, 'dp')
- norm_square: float32 [4, 768], P(None, 'dp')
- norm_value: float32 [4, 768], P(None, 'dp')
- norm_grad: float32 [4, 768], P(None, 'dp')
Inputs may be any that keep to these rules, and one draw needn't show every extreme that they name: `segments`: along each packed row of 128 positions the segment numbers never fall, and a segment holds at most 64 positions.
All inputs are finite; a program needn't handle non-finite values.
Results may differ from a plain program's by a relative error of at most 0.02.
Values may be sent and summed in bfloat16 or wider, within the bound.
A program may use at most 128 MiB of HBM per device.

v0:
```python
import jax
import jax.numpy as jnp
from jax import lax
from jax.sharding import PartitionSpec as P

HEAD = 64
MICRO = 2
STEP = 10


NORM_EPS = 1e-05
CLIP_AT = 1.0
BETA_ONE = 0.9
BETA_TWO = 0.95
ADAM_EPS = 1e-08
WEIGHT_DECAY = 0.01
RATE_MATRIX = 0.05
RATE_OUT = 0.3
RATE_VECTOR = 0.5


def norm_parts(values, gain, shift):
    center = jnp.mean(values, axis=-1, keepdims=True)
    offset = values - center
    spread = jnp.mean(offset * offset, axis=-1, keepdims=True)
    inverse = lax.rsqrt(spread + NORM_EPS)
    scaled = offset * inverse
    return (scaled * gain + shift, scaled, inverse)


def norm_back(grad_rows, scaled, inverse, gain):
    through = grad_rows * gain
    first_mean = jnp.mean(through, axis=-1, keepdims=True)
    second_mean = jnp.mean(through * scaled, axis=-1, keepdims=True)
    grad_in = inverse * (through - first_mean - scaled * second_mean)
    return (grad_in, jnp.sum(grad_rows * scaled, axis=0), jnp.sum(grad_rows, axis=0))


def left_product(first_arr, second_arr):
    return lax.dot_general(
        first_arr, second_arr, (((0,), (0,)), ((), ())), preferred_element_type=jnp.float32
    )


def right_product(first_arr, second_arr):
    return lax.dot_general(
        first_arr, second_arr, (((1,), (1,)), ((), ())), preferred_element_type=jnp.float32
    )


def exact_gelu(values):
    return jax.nn.gelu(values, approximate=False)


def masked_scores(queries, key_rows, allowed):
    scaling = HEAD ** (-0.5)
    scores = (
        jnp.einsum("bqhe,bkhe->bhqk", queries, key_rows, preferred_element_type=jnp.float32)
        * scaling
    )
    return jnp.where(allowed, scores, -1e30)


def micro_pass(gathered, tokens_part, time_part, labels, grad_rows):
    w_qkv, w_out, w_up, w_down, norm_low = gathered
    gain_rows = norm_low.astype(jnp.float32)
    seq_count, length = labels.shape
    row_count = seq_count * length
    local_width = w_qkv.shape[2]
    local_heads = local_width // HEAD
    scaling = HEAD ** (-0.5)
    start_rows = tokens_part.astype(jnp.float32) + jnp.repeat(
        time_part.astype(jnp.float32), length, axis=0
    )
    normed, scaled_one, inverse_one = norm_parts(start_rows, gain_rows[0], gain_rows[1])
    normed = normed.astype(jnp.bfloat16)
    project = jnp.einsum("td,cdf->ctf", normed, w_qkv, preferred_element_type=jnp.float32).astype(
        jnp.bfloat16
    )
    shaped = project.reshape(3, seq_count, length, local_heads, HEAD)
    queries, key_rows, value_rows = (shaped[0], shaped[1], shaped[2])
    allowed = labels[:, None, :, None] == labels[:, None, None, :]
    scores = masked_scores(queries, key_rows, allowed)
    highest = jnp.max(scores, axis=-1, keepdims=True)
    exponent = jnp.exp(scores - highest)
    totals = jnp.sum(exponent, axis=-1, keepdims=True)
    weights_low = (exponent / totals).astype(jnp.bfloat16)
    log_total = highest + jnp.log(totals)
    mixed_heads = jnp.einsum(
        "bhqk,bkhe->bqhe", weights_low, value_rows, preferred_element_type=jnp.float32
    )
    mixed_heads = mixed_heads.astype(jnp.bfloat16).reshape(row_count, local_width)
    attn_part = jnp.dot(mixed_heads, w_out, preferred_element_type=jnp.float32)
    middle = start_rows + lax.psum(attn_part, "mp")
    normed_two, scaled_two, inverse_two = norm_parts(middle, gain_rows[2], gain_rows[3])
    normed_two = normed_two.astype(jnp.bfloat16)
    before = jnp.dot(normed_two, w_up, preferred_element_type=jnp.float32)
    active, gelu_pull = jax.vjp(exact_gelu, before)
    active = active.astype(jnp.bfloat16)
    mlp_part = jnp.dot(active, w_down, preferred_element_type=jnp.float32)
    result = middle + lax.psum(mlp_part.astype(jnp.bfloat16), "mp").astype(jnp.float32)
    grad_down = left_product(active, grad_rows)
    grad_active = right_product(grad_rows, w_down)
    (grad_before,) = gelu_pull(grad_active)
    grad_before = grad_before.astype(jnp.bfloat16)
    grad_up = left_product(normed_two, grad_before)
    normed_two_part = right_product(grad_before, w_up)
    grad_normed_two = lax.psum(normed_two_part, "mp")
    back_two, gain_two, shift_two = norm_back(
        grad_normed_two, scaled_two, inverse_two, gain_rows[2]
    )
    grad_middle = grad_rows.astype(jnp.float32) + back_two
    branch_low = grad_middle.astype(jnp.bfloat16)
    grad_out = left_product(mixed_heads, branch_low)
    grad_mixed = right_product(branch_low, w_out).astype(jnp.bfloat16)
    grad_mixed = grad_mixed.reshape(seq_count, length, local_heads, HEAD)
    probs_full = jnp.exp(masked_scores(queries, key_rows, allowed) - log_total)
    probs_low = probs_full.astype(jnp.bfloat16)
    grad_value = jnp.einsum(
        "bhqk,bqhe->bkhe", probs_low, grad_mixed, preferred_element_type=jnp.float32
    ).astype(jnp.bfloat16)
    grad_probs = jnp.einsum(
        "bqhe,bkhe->bhqk", grad_mixed, value_rows, preferred_element_type=jnp.float32
    )
    row_inner = jnp.sum(grad_probs * probs_full, axis=-1, keepdims=True)
    grad_scores = (probs_full * (grad_probs - row_inner)).astype(jnp.bfloat16)
    grad_query = (
        jnp.einsum("bhqk,bkhe->bqhe", grad_scores, key_rows, preferred_element_type=jnp.float32)
        * scaling
    ).astype(jnp.bfloat16)
    grad_key = (
        jnp.einsum("bhqk,bqhe->bkhe", grad_scores, queries, preferred_element_type=jnp.float32)
        * scaling
    ).astype(jnp.bfloat16)
    grad_project = jnp.stack([grad_query, grad_key, grad_value]).reshape(3, row_count, local_width)
    grad_qkv = jnp.einsum("td,ctf->cdf", normed, grad_project, preferred_element_type=jnp.float32)
    normed_part = jnp.einsum("ctf,cdf->td", grad_project, w_qkv, preferred_element_type=jnp.float32)
    grad_normed = lax.psum(normed_part.astype(jnp.bfloat16), "mp").astype(jnp.float32)
    back_one, gain_one, shift_one = norm_back(grad_normed, scaled_one, inverse_one, gain_rows[0])
    grad_start = grad_middle + back_one
    grad_norm_rows = jnp.stack([gain_one, shift_one, gain_two, shift_two])
    return (
        result.astype(jnp.bfloat16),
        grad_start.astype(jnp.bfloat16),
        (grad_qkv, grad_out, grad_up, grad_down, grad_norm_rows),
    )


def adam_step(weight, gradient, moment, second, step_rate, decay_rate):
    moment = BETA_ONE * moment + (1.0 - BETA_ONE) * gradient
    second = BETA_TWO * second + (1.0 - BETA_TWO) * gradient * gradient
    moment_hat = moment / (1.0 - BETA_ONE**STEP)
    second_hat = second / (1.0 - BETA_TWO**STEP)
    weight = weight - step_rate * (
        moment_hat / (jnp.sqrt(second_hat) + ADAM_EPS) + decay_rate * weight
    )
    return (moment, second, weight)


def body(
    tokens,
    time_emb,
    segments,
    cotangent,
    w_qkv,
    w_out,
    w_up,
    w_down,
    norm_params,
    qkv_first,
    qkv_second,
    out_first,
    out_second,
    up_first,
    up_second,
    down_first,
    down_second,
    norm_first,
    norm_second,
):
    qkv_low = w_qkv.astype(jnp.bfloat16)
    out_low = w_out.astype(jnp.bfloat16)
    up_low = w_up.astype(jnp.bfloat16)
    down_low = w_down.astype(jnp.bfloat16)
    norm_low = norm_params.astype(jnp.bfloat16)
    rows_each = tokens.shape[0] // MICRO
    seqs_each = segments.shape[0] // MICRO
    outputs = []
    input_grads = []
    for micro_index in range(MICRO):
        gathered = (
            lax.all_gather(qkv_low, "dp", axis=1, tiled=True),
            lax.all_gather(out_low, "dp", axis=1, tiled=True),
            lax.all_gather(up_low, "dp", axis=0, tiled=True),
            lax.all_gather(down_low, "dp", axis=1, tiled=True),
            lax.all_gather(norm_low, "dp", axis=1, tiled=True),
        )
        first_row = micro_index * rows_each
        first_seq = micro_index * seqs_each
        result, grad_start, grads_local = micro_pass(
            gathered,
            tokens[first_row : first_row + rows_each],
            time_emb[first_seq : first_seq + seqs_each],
            segments[first_seq : first_seq + seqs_each],
            cotangent[first_row : first_row + rows_each],
        )
        outputs.append(result)
        input_grads.append(grad_start)
        reduced_part = (
            lax.psum_scatter(
                grads_local[0].astype(jnp.bfloat16), "dp", scatter_dimension=1, tiled=True
            ).astype(jnp.float32),
            lax.psum_scatter(
                grads_local[1].astype(jnp.bfloat16), "dp", scatter_dimension=1, tiled=True
            ).astype(jnp.float32),
            lax.psum_scatter(
                grads_local[2].astype(jnp.bfloat16), "dp", scatter_dimension=0, tiled=True
            ).astype(jnp.float32),
            lax.psum_scatter(
                grads_local[3].astype(jnp.bfloat16), "dp", scatter_dimension=1, tiled=True
            ).astype(jnp.float32),
            lax.psum_scatter(
                grads_local[4].astype(jnp.bfloat16), "dp", scatter_dimension=1, tiled=True
            ).astype(jnp.float32),
        )
        shares = reduced_part if micro_index == 0 else jax.tree.map(jnp.add, shares, reduced_part)
    mp_count = lax.axis_size("mp")
    squares = jnp.sum(shares[4] * shares[4]) / mp_count
    for grad_part in shares[:4]:
        squares = squares + jnp.sum(grad_part * grad_part)
    grad_norm = jnp.sqrt(lax.psum(squares, ("dp", "mp")))
    factor = jnp.minimum(1.0, CLIP_AT / (grad_norm + 1e-06))
    norm_grad = shares[4] * factor
    qkv_new = adam_step(w_qkv, shares[0] * factor, qkv_first, qkv_second, RATE_MATRIX, WEIGHT_DECAY)
    out_new = adam_step(w_out, shares[1] * factor, out_first, out_second, RATE_OUT, WEIGHT_DECAY)
    up_new = adam_step(w_up, shares[2] * factor, up_first, up_second, RATE_MATRIX, WEIGHT_DECAY)
    down_new = adam_step(
        w_down, shares[3] * factor, down_first, down_second, RATE_MATRIX, WEIGHT_DECAY
    )
    norm_new = adam_step(norm_params, norm_grad, norm_first, norm_second, RATE_VECTOR, 0.0)
    return (
        jnp.concatenate(outputs, axis=0),
        jnp.concatenate(input_grads, axis=0),
        grad_norm,
        qkv_new[0],
        qkv_new[1],
        qkv_new[2],
        out_new[0],
        out_new[1],
        out_new[2],
        up_new[0],
        up_new[1],
        up_new[2],
        down_new[0],
        down_new[1],
        down_new[2],
        norm_new[0],
        norm_new[1],
        norm_new[2],
        norm_grad,
    )


def solution(mesh):
    return jax.shard_map(
        body,
        mesh=mesh,
        in_specs=(
            P("dp", None),
            P("dp", None),
            P("dp", None),
            P("dp", None),
            P(None, "dp", "mp"),
            P("mp", "dp"),
            P("dp", "mp"),
            P("mp", "dp"),
            P(None, "dp"),
            P(None, "dp", "mp"),
            P(None, "dp", "mp"),
            P("mp", "dp"),
            P("mp", "dp"),
            P("dp", "mp"),
            P("dp", "mp"),
            P("mp", "dp"),
            P("mp", "dp"),
            P(None, "dp"),
            P(None, "dp"),
        ),
        out_specs=(
            P("dp", None),
            P("dp", None),
            P(),
            P(None, "dp", "mp"),
            P(None, "dp", "mp"),
            P(None, "dp", "mp"),
            P("mp", "dp"),
            P("mp", "dp"),
            P("mp", "dp"),
            P("dp", "mp"),
            P("dp", "mp"),
            P("dp", "mp"),
            P("mp", "dp"),
            P("mp", "dp"),
            P("mp", "dp"),
            P(None, "dp"),
            P(None, "dp"),
            P(None, "dp"),
            P(None, "dp"),
        ),
        check_vma=False,
    )
```

profile of v0, /device:TPU:1, one launch (start us, length us, event | category | flops | bytes accessed | tf_op | source)
XLA Modules:
  0.0 1215.4 jit_solution(9350677642299469655)
XLA Ops:
  13.4 25.8 %all-gather = bf16[32,24,4]{1,2,0:T(4,128)(2,1)S(1)} all-gather(bf16[1,24,4]{1,2,0:T(4,128)(2,1)S(1)} %convert_bitcast_fusion), channel_id=1, replica_groups=mesh['dp'=32,'mp'=4] {'dp'}, dimensions={0}, use_global_device_ids=true | all-gather | bytes 6336 | tf_op jit(solution)/shard_map/all_gather | solution.py:196
  39.6 24.6 %all_gather.21 = bf16[3,768,192]{2,1,0:T(8,128)(2,1)S(1)} all-gather(bf16[3,24,192]{2,1,0:T(8,128)(2,1)S(1)} %convert_element_type.254), channel_id=1, replica_groups=mesh['dp'=32,'mp'=4] {'dp'}, dimensions={1}, use_global_device_ids=true | all-gather | bytes 912384 | tf_op jit(solution)/shard_map/all_gather | solution.py:192
  70.1 22.8 %all_gather.22 = bf16[192,768]{0,1:T(8,128)(2,1)S(1)} all-gather(bf16[192,24]{0,1:T(8,128)(2,1)S(1)} %convert_element_type.260), channel_id=1, replica_groups=mesh['dp'=32,'mp'=4] {'dp'}, dimensions={1}, use_global_device_ids=true | all-gather | bytes 304128 | tf_op jit(solution)/shard_map/all_gather | solution.py:193
  104.2 123.9 %all-reduce.16.cloned.1.call-done = (f32[1024,768]{1,0:T(8,128)}, f32[1024,768]{1,0:T(8,128)}) async-done(((f32[1024,768]{1,0:T(8,128)}, f32[1024,768]{1,0:T(8,128)}), (f32[1024,768]{1,0:T(8,128)}, f32[1024,768]{1,0:T(8,128)})) %all-reduce.16.cloned.1.call-update) | async-done | bytes 6291472 | tf_op jit(solution)/shard_map/psum | solution.py:94
  237.1 11.0 multiply_convert_fusion.1
  248.0 9.7 multiply_convert_fusion
  257.8 5.3 add_convert_fusion.1
  274.4 4.3 convolution_convert_fusion.5
  279.0 4.4 convolution_convert_fusion.4
  283.4 4.1 convolution_convert_fusion.3
  293.7 4.5 convolution_convert_fusion
  298.2 103.5 %all-reduce.14.cloned.1.call-done = (f32[1024,768]{1,0:T(8,128)}, f32[1024,768]{1,0:T(8,128)}) async-done(((f32[1024,768]{1,0:T(8,128)}, f32[1024,768]{1,0:T(8,128)}), (f32[1024,768]{1,0:T(8,128)}, f32[1024,768]{1,0:T(8,128)})) %all-reduce.14.cloned.1.call-update) | async-done | bytes 6291472 | tf_op jit(solution)/shard_map/psum | solution.py:108
  401.7 5.8 multiply_reduce_fusion.1
  455.3 4.0 convolution_convert_fusion.1
  462.1 3.9 bitcast_convert_fusion
  469.4 40.7 %reduce-scatter.17.cloned.1.call-done = bf16[768,24]{0,1:T(8,128)(2,1)} async-done(((bf16[768,768]{0,1:T(8,128)(2,1)}), bf16[768,24]{0,1:T(8,128)(2,1)}) %reduce-scatter.17.cloned.1.call-update) | async-done | bytes 36880 | tf_op jit(solution)/shard_map/reduce_scatter | solution.py:219
  510.1 78.7 %reduce-scatter.19.cloned.1.call-done = bf16[768,24]{0,1:T(8,128)(2,1)} async-done(((bf16[768,768]{0,1:T(8,128)(2,1)}), bf16[768,24]{0,1:T(8,128)(2,1)}) %reduce-scatter.19.cloned.1.call-update) | async-done | bytes 36880 | tf_op jit(solution)/shard_map/reduce_scatter | solution.py:219
  590.2 76.0 %reduce-scatter.9.cloned.1.call-done = bf16[192,24]{0,1:T(8,128)(2,1)} async-done(((bf16[192,768]{0,1:T(8,128)(2,1)}), bf16[192,24]{0,1:T(8,128)(2,1)}) %reduce-scatter.9.cloned.1.call-update) | async-done | bytes 9232 | tf_op jit(solution)/shard_map/reduce_scatter | solution.py:213
  666.3 77.3 %reduce-scatter.11.cloned.1.call-done = bf16[192,24]{0,1:T(8,128)(2,1)} async-done(((bf16[192,768]{0,1:T(8,128)(2,1)}), bf16[192,24]{0,1:T(8,128)(2,1)}) %reduce-scatter.11.cloned.1.call-update) | async-done | bytes 9232 | tf_op jit(solution)/shard_map/reduce_scatter | solution.py:213
  744.9 112.5 %all-reduce.18.cloned.1.call-done = (bf16[3,768,192]{2,0,1:T(4,128)(2,1)}, bf16[3,768,192]{2,0,1:T(4,128)(2,1)}) async-done(((bf16[3,768,192]{2,0,1:T(4,128)(2,1)}, bf16[3,768,192]{2,0,1:T(4,128)(2,1)}), (bf16[3,768,192]{2,0,1:T(4,128)(2,1)}, bf16[3,768,192]{2,0,1:T(4,128)(2,1)})) %all-reduce.18.cloned.1.call-update) | async-done | bytes 1769488
  859.7 127.3 %all-reduce.20.cloned.1.call-done = (bf16[1024,768]{1,0:T(8,128)(2,1)}, bf16[1024,768]{1,0:T(8,128)(2,1)}, bf16[1024,768]{1,0:T(8,128)(2,1)}, bf16[1024,768]{1,0:T(8,128)(2,1)}) async-done(((bf16[1024,768]{1,0:T(8,128)(2,1)}, bf16[1024,768]{1,0:T(8,128)(2,1)}, bf16[1024,768]{1,0:T(8,128)(2,1)}, bf16[1024,768]{1,0:T(8,128)(2,1)}), (bf16[1024,768]{1,0:T(8,128)(2,1)}, bf16[1024,768]{1,0:T(8,128)(2,1)}, ...) | async-done | bytes 6291472 | tf_op jit(solution)/shard_map/psum | solution.py:101
  987.1 4.7 fusion.11
  995.2 123.1 %all-reduce.6 = (bf16[4,768]{1,0:T(4,128)(2,1)S(1)}, bf16[4,768]{1,0:T(4,128)(2,1)S(1)}) all-reduce(bf16[4,768]{1,0:T(4,128)(2,1)S(1)} %pad_maximum_fusion.2, bf16[4,768]{1,0:T(4,128)(2,1)S(1)} %pad_maximum_fusion.3), channel_id=2, replica_groups=mesh['dp'=32,'mp'=4] {'dp'}, use_global_device_ids=true, to_apply=%region_34.35.clone | all-reduce | flops 6144 | bytes 24576
  1122.3 67.5 %psum.71 = f32[]{:T(128)} all-reduce(f32[]{:T(128)S(6)} %add.285), channel_id=1, replica_groups=mesh['dp'=32,'mp'=4] {'dp','mp'}, use_global_device_ids=true, to_apply=%region_53.54 | all-reduce | flops 1 | bytes 8 | tf_op jit(solution)/shard_map/psum | solution.py:231
  (392 shorter events, 126.5 us)
Async XLA Ops:
  8.0 220.0 %all-reduce.16.cloned.1.call-start = ((), (), s32[]{:S(2)}) async-start(), calls=%async_computation.15 | async-start | bytes 12582912 | tf_op jit(solution)/shard_map/psum | solution.py:94
  39.5 193.4 %copy-start.78 = (f32[768]{0:T(1024)}, f32[768]{0:T(1024)S(1)}, u32[]{:S(2)}) copy-start(f32[768]{0:T(1024)S(1)} %get-tuple-element.96) | copy-start | bytes 9220
  101.0 136.1 %all-gather.4.cloned.1.call-start = ((), (), s32[]{:S(2)}) async-start(), calls=%async_computation.6 | async-start | bytes 1216512 | tf_op jit(solution)/shard_map/all_gather | solution.py:194
  102.5 155.3 %all-gather.6.cloned.1.call-start = ((), (), s32[]{:S(2)}) async-start(), calls=%async_computation.7 | async-start | bytes 1216512 | tf_op jit(solution)/shard_map/all_gather | solution.py:195
  104.1 297.5 %all-reduce.14.cloned.1.call-start = ((), (), s32[]{:S(2)}) async-start(), calls=%async_computation.14 | async-start | bytes 12582912 | tf_op jit(solution)/shard_map/psum | solution.py:108
  274.4 193.6 %reduce-scatter.13.cloned.1.call-start = ((), (), s32[]{:S(2)}) async-start(), calls=%async_computation.10 | async-start | bytes 1216512 | tf_op jit(solution)/shard_map/reduce_scatter | solution.py:216
  278.8 189.2 %reduce-scatter.15.cloned.1.call-start = ((), (), s32[]{:S(2)}) async-start(), calls=%async_computation.11 | async-start | bytes 1216512 | tf_op jit(solution)/shard_map/reduce_scatter | solution.py:216
  283.4 226.7 %reduce-scatter.17.cloned.1.call-start = ((), (), s32[]{:S(2)}) async-start(), calls=%async_computation.12 | async-start | bytes 1216512 | tf_op jit(solution)/shard_map/reduce_scatter | solution.py:219
  287.6 301.2 %reduce-scatter.19.cloned.1.call-start = ((), (), s32[]{:S(2)}) async-start(), calls=%async_computation.13 | async-start | bytes 1216512 | tf_op jit(solution)/shard_map/reduce_scatter | solution.py:219
  293.7 372.6 %reduce-scatter.9.cloned.1.call-start = ((), (), s32[]{:S(2)}) async-start(), calls=%async_computation.8 | async-start | bytes 405504 | tf_op jit(solution)/shard_map/reduce_scatter | solution.py:213
  442.1 301.4 %reduce-scatter.11.cloned.1.call-start = ((), (), s32[]{:S(2)}) async-start(), calls=%async_computation.9 | async-start | bytes 405504 | tf_op jit(solution)/shard_map/reduce_scatter | solution.py:213
  447.8 409.6 %all-reduce.18.cloned.1.call-start = ((), (), s32[]{:S(2)}) async-start(), calls=%async_computation.16 | async-start | bytes 6291456
  454.1 532.9 %all-reduce.20.cloned.1.call-start = ((), (), s32[]{:S(2)}) async-start(), calls=%async_computation.17 | async-start | bytes 12582912 | tf_op jit(solution)/shard_map/psum | solution.py:101
  466.0 124.2 %copy-start.101 = (bf16[768]{0:T(1024)(128)(2,1)S(1)}, bf16[768]{0:T(1024)(128)(2,1)}, u32[]{:S(2)}) copy-start(bf16[768]{0:T(1024)(128)(2,1)} %get-tuple-element.156) | copy-start | bytes 4612
  466.0 124.2 %copy-start.100 = (bf16[768]{0:T(1024)(128)(2,1)S(1)}, bf16[768]{0:T(1024)(128)(2,1)}, u32[]{:S(2)}) copy-start(bf16[768]{0:T(1024)(128)(2,1)} %get-tuple-element.78) | copy-start | bytes 4612
  466.0 124.2 %copy-start.99 = (bf16[768]{0:T(1024)(128)(2,1)S(1)}, bf16[768]{0:T(1024)(128)(2,1)}, u32[]{:S(2)}) copy-start(bf16[768]{0:T(1024)(128)(2,1)} %get-tuple-element.89) | copy-start | bytes 4612
  466.0 521.0 %copy-start.1 = (bf16[2048,768]{1,0:T(8,128)(2,1)S(1)}, bf16[2048,768]{1,0:T(8,128)(2,1)}, u32[]{:S(2)}) copy-start(bf16[2048,768]{1,0:T(8,128)(2,1)} %param.19) | copy-start | bytes 9437188
  466.0 521.0 %copy-start.46 = (f32[8,768]{1,0:T(8,128)S(1)}, f32[8,768]{1,0:T(8,128)}, u32[]{:S(2)}) copy-start(f32[8,768]{1,0:T(8,128)} %copy-done.45) | copy-start | bytes 73732
  466.0 521.0 %copy-start.48 = (f32[8,768]{1,0:T(8,128)S(1)}, f32[8,768]{1,0:T(8,128)}, u32[]{:S(2)}) copy-start(f32[8,768]{1,0:T(8,128)} %copy-done.47) | copy-start | bytes 73732
  466.1 521.0 %copy-start.67 = (f32[1024]{0:T(1024)S(1)}, f32[1024]{0:T(1024)}, u32[]{:S(2)}) copy-start(f32[1024]{0:T(1024)} %copy-done.66) | copy-start | bytes 12292
  466.1 521.0 %copy-start.69 = (f32[1024]{0:T(1024)S(1)}, f32[1024]{0:T(1024)}, u32[]{:S(2)}) copy-start(f32[1024]{0:T(1024)} %copy-done.68) | copy-start | bytes 12292
  466.1 521.0 %copy-start.85 = (f32[768]{0:T(1024)S(1)}, f32[768]{0:T(1024)}, u32[]{:S(2)}) copy-start(f32[768]{0:T(1024)} %copy-done.84) | copy-start | bytes 9220
  466.1 521.0 %copy-start.87 = (f32[1024]{0:T(1024)S(1)}, f32[1024]{0:T(1024)}, u32[]{:S(2)}) copy-start(f32[1024]{0:T(1024)} %copy-done.86) | copy-start | bytes 12292
  466.1 521.0 %copy-start.89 = (f32[1024]{0:T(1024)S(1)}, f32[1024]{0:T(1024)}, u32[]{:S(2)}) copy-start(f32[1024]{0:T(1024)} %copy-done.88) | copy-start | bytes 12292
  (105 other events, 1051.0 us)
Sparse Core Ops, SparseCore 0:
  101.1 126.9 all-reduce.15
  274.5 127.1 all-reduce.13
Sparse Core Ops, SparseCore 1:
  104.3 42.9 all-gather.3
  150.0 42.2 all-gather.5
  278.8 74.0 reduce-scatter.12
  356.5 74.9 reduce-scatter.14
  435.0 75.1 reduce-scatter.16
  513.7 75.0 reduce-scatter.18
  592.1 74.1 reduce-scatter.8
  669.6 73.9 reduce-scatter.10
  746.8 110.6 all-reduce.17
  860.1 126.9 all-reduce.19
where the time goes:
time: 1220 us
  waiting for transfers between devices  740 us (61%)
  blocking collectives  264 us (22%)
  matrix products  92.8 us (8%)
  other arithmetic  58.7 us (5%)
  local copies, waits for them, and re-layouts  35.5 us (3%)
  between operations  23.5 us (2%)
    reduce_scatter x2, waiting for transfers between devices, body(): lax.psum_scatter(grads_local[1].astype(jnp.bfloat16), 'dp', scatter_dimen...  153 us
    psum x1, waiting for transfers between devices, micro_pass(): lax.psum(mlp_part.astype(jnp.bfloat16), 'mp').astype(jnp.float32)  127 us
    psum x1, waiting for transfers between devices, micro_pass(): middle = start_rows + lax.psum(attn_part, 'mp')  124 us
    unnamed x1, blocking collectives  123 us
    reduce_scatter x2, waiting for transfers between devices, body(): lax.psum_scatter(grads_local[3].astype(jnp.bfloat16), 'dp', scatter_dimen...  119 us
    unnamed x13, waiting for transfers between devices  113 us
    psum x1, waiting for transfers between devices, micro_pass(): grad_normed_two = lax.psum(normed_two_part, 'mp')  103 us
    psum x1, blocking collectives, body(): grad_norm = jnp.sqrt(lax.psum(squares, ('dp', 'mp')))  67.5 us
  transfers between devices with their start and end apart: 12, of which 8 were waited for; matrix products, arithmetic and copies ran while one was open for 10% of the time, Pallas kernels for 0%

commit v1 on v0

v1 whole, which is shorter than its diff:
```python
import jax
import jax.numpy as jnp
from jax import lax
from jax.sharding import PartitionSpec as P

HEAD = 64
QKV = 192
HIDDEN = 768
STEP = 10


NORM_EPS = 1e-05
CLIP_AT = 1.0
BETA_ONE = 0.9
BETA_TWO = 0.95
ADAM_EPS = 1e-08
WEIGHT_DECAY = 0.01
RATE_MATRIX = 0.05
RATE_OUT = 0.3
RATE_VECTOR = 0.5


def norm_parts(values, gain, shift):
    center = jnp.mean(values, axis=-1, keepdims=True)
    offset = values - center
    spread = jnp.mean(offset * offset, axis=-1, keepdims=True)
    inverse = lax.rsqrt(spread + NORM_EPS)
    scaled = offset * inverse
    return (scaled * gain + shift, scaled, inverse)


def norm_back(grad_rows, scaled, inverse, gain):
    through = grad_rows * gain
    first_mean = jnp.mean(through, axis=-1, keepdims=True)
    second_mean = jnp.mean(through * scaled, axis=-1, keepdims=True)
    grad_in = inverse * (through - first_mean - scaled * second_mean)
    return (grad_in, jnp.sum(grad_rows * scaled, axis=0), jnp.sum(grad_rows, axis=0))


def left_product(first_arr, second_arr):
    return lax.dot_general(
        first_arr, second_arr, (((0,), (0,)), ((), ())), preferred_element_type=jnp.float32
    )


def right_product(first_arr, second_arr):
    return lax.dot_general(
        first_arr, second_arr, (((1,), (1,)), ((), ())), preferred_element_type=jnp.float32
    )


def exact_gelu(values):
    return jax.nn.gelu(values, approximate=False)


def masked_scores(queries, key_rows, allowed):
    scaling = HEAD ** (-0.5)
    scores = (
        jnp.einsum("bqhe,bkhe->bhqk", queries, key_rows, preferred_element_type=jnp.float32)
        * scaling
    )
    return jnp.where(allowed, scores, -1e30)


def layer_pass(weights, gain_rows, tokens_part, time_part, labels, grad_rows):
    seq_count, length = labels.shape
    row_count = seq_count * length
    blocks = weights.shape[0]
    model = weights.shape[1]
    w_qkv = weights[:, :, : 3 * QKV].reshape(blocks, model, 3, QKV)
    w_out = weights[:, :, 3 * QKV : 4 * QKV]
    w_up = weights[:, :, 4 * QKV : 4 * QKV + HIDDEN]
    w_down = weights[:, :, 4 * QKV + HIDDEN :]
    scaling = HEAD ** (-0.5)
    heads = QKV // HEAD
    start_rows = tokens_part.astype(jnp.float32) + jnp.repeat(
        time_part.astype(jnp.float32), length, axis=0
    )
    normed, scaled_one, inverse_one = norm_parts(start_rows, gain_rows[0], gain_rows[1])
    normed = normed.astype(jnp.bfloat16)
    project = jnp.einsum(
        "td,mdcf->cmtf", normed, w_qkv, preferred_element_type=jnp.float32
    ).astype(jnp.bfloat16)
    shaped = project.reshape(3, blocks, seq_count, length, heads, HEAD)
    queries, key_rows, value_rows = (shaped[0], shaped[1], shaped[2])
    allowed = labels[:, :, None] == labels[:, None, :]
    allowed = allowed[None, :, None, :, :]
    scores = (
        jnp.einsum("mbqhe,mbkhe->mbhqk", queries, key_rows, preferred_element_type=jnp.float32)
        * scaling
    )
    scores = jnp.where(allowed, scores, -1e30)
    highest = jnp.max(scores, axis=-1, keepdims=True)
    exponent = jnp.exp(scores - highest)
    totals = jnp.sum(exponent, axis=-1, keepdims=True)
    probs_full = exponent / totals
    probs_low = probs_full.astype(jnp.bfloat16)
    mixed_heads = jnp.einsum(
        "mbhqk,mbkhe->mbqhe", probs_low, value_rows, preferred_element_type=jnp.float32
    )
    mixed_heads = mixed_heads.astype(jnp.bfloat16).reshape(blocks, row_count, QKV)
    middle = start_rows + jnp.einsum(
        "mtf,mdf->td", mixed_heads, w_out, preferred_element_type=jnp.float32
    )
    normed_two, scaled_two, inverse_two = norm_parts(middle, gain_rows[2], gain_rows[3])
    normed_two = normed_two.astype(jnp.bfloat16)
    before = jnp.einsum("td,mdf->mtf", normed_two, w_up, preferred_element_type=jnp.float32)
    active, gelu_pull = jax.vjp(exact_gelu, before)
    active = active.astype(jnp.bfloat16)
    result = middle + jnp.einsum(
        "mtf,mdf->td", active, w_down, preferred_element_type=jnp.float32
    )
    grad_down = jnp.einsum("td,mtf->mdf", grad_rows, active, preferred_element_type=jnp.float32)
    grad_active = jnp.einsum("td,mdf->mtf", grad_rows, w_down, preferred_element_type=jnp.float32)
    (grad_before,) = gelu_pull(grad_active)
    grad_before = grad_before.astype(jnp.bfloat16)
    grad_up = jnp.einsum("td,mtf->mdf", normed_two, grad_before, preferred_element_type=jnp.float32)
    grad_normed_two = jnp.einsum(
        "mtf,mdf->td", grad_before, w_up, preferred_element_type=jnp.float32
    )
    back_two, gain_two, shift_two = norm_back(
        grad_normed_two, scaled_two, inverse_two, gain_rows[2]
    )
    grad_middle = grad_rows.astype(jnp.float32) + back_two
    branch_low = grad_middle.astype(jnp.bfloat16)
    grad_out = jnp.einsum(
        "td,mtf->mdf", branch_low, mixed_heads, preferred_element_type=jnp.float32
    )
    grad_mixed = jnp.einsum(
        "td,mdf->mtf", branch_low, w_out, preferred_element_type=jnp.float32
    ).astype(jnp.bfloat16)
    grad_mixed = grad_mixed.reshape(blocks, seq_count, length, heads, HEAD)
    grad_value = jnp.einsum(
        "mbhqk,mbqhe->mbkhe", probs_low, grad_mixed, preferred_element_type=jnp.float32
    ).astype(jnp.bfloat16)
    grad_probs = jnp.einsum(
        "mbqhe,mbkhe->mbhqk", grad_mixed, value_rows, preferred_element_type=jnp.float32
    )
    row_inner = jnp.sum(grad_probs * probs_full, axis=-1, keepdims=True)
    grad_scores = (probs_full * (grad_probs - row_inner)).astype(jnp.bfloat16)
    grad_query = (
        jnp.einsum("mbhqk,mbkhe->mbqhe", grad_scores, key_rows, preferred_element_type=jnp.float32)
        * scaling
    ).astype(jnp.bfloat16)
    grad_key = (
        jnp.einsum("mbhqk,mbqhe->mbkhe", grad_scores, queries, preferred_element_type=jnp.float32)
        * scaling
    ).astype(jnp.bfloat16)
    grad_project = jnp.stack([grad_query, grad_key, grad_value]).reshape(
        3, blocks, row_count, QKV
    )
    grad_qkv = jnp.einsum(
        "td,cmtf->mdcf", normed, grad_project, preferred_element_type=jnp.float32
    ).reshape(blocks, model, 3 * QKV)
    grad_normed = jnp.einsum(
        "cmtf,mdcf->td", grad_project, w_qkv, preferred_element_type=jnp.float32
    )
    back_one, gain_one, shift_one = norm_back(grad_normed, scaled_one, inverse_one, gain_rows[0])
    grad_start = grad_middle + back_one
    grad_norm_rows = jnp.stack([gain_one, shift_one, gain_two, shift_two])
    grads = jnp.concatenate([grad_qkv, grad_out, grad_up, grad_down], axis=2)
    return (
        result.astype(jnp.bfloat16),
        grad_start.astype(jnp.bfloat16),
        grads.astype(jnp.bfloat16),
        grad_norm_rows,
    )


def adam_step(weight, gradient, moment, second, step_rate, decay_rate):
    moment = BETA_ONE * moment + (1.0 - BETA_ONE) * gradient
    second = BETA_TWO * second + (1.0 - BETA_TWO) * gradient * gradient
    moment_hat = moment / (1.0 - BETA_ONE**STEP)
    second_hat = second / (1.0 - BETA_TWO**STEP)
    weight = weight - step_rate * (
        moment_hat / (jnp.sqrt(second_hat) + ADAM_EPS) + decay_rate * weight
    )
    return (moment, second, weight)


def body(
    tokens,
    time_emb,
    segments,
    cotangent,
    w_qkv,
    w_out,
    w_up,
    w_down,
    norm_params,
    qkv_first,
    qkv_second,
    out_first,
    out_second,
    up_first,
    up_second,
    down_first,
    down_second,
    norm_first,
    norm_second,
):
    low = jnp.bfloat16
    packed = jnp.concatenate(
        [w_qkv[0], w_qkv[1], w_qkv[2], w_out.T, w_up, w_down.T], axis=1
    ).astype(low)
    weights = lax.all_gather(packed, "mp", axis=0)
    weights = lax.all_gather(weights, "dp", axis=1, tiled=True)
    gain_rows = lax.all_gather(norm_params.astype(low), "dp", axis=1, tiled=True)
    gain_rows = gain_rows.astype(jnp.float32)
    place = lax.axis_index("mp")
    seqs = segments.shape[0] // lax.axis_size("mp")
    rows = tokens.shape[0] // lax.axis_size("mp")
    result, grad_start, grads, grad_norm_rows = layer_pass(
        weights,
        gain_rows,
        lax.dynamic_slice_in_dim(tokens, place * rows, rows),
        lax.dynamic_slice_in_dim(time_emb, place * seqs, seqs),
        lax.dynamic_slice_in_dim(segments, place * seqs, seqs),
        lax.dynamic_slice_in_dim(cotangent, place * rows, rows),
    )
    result = lax.all_gather(result, "mp", axis=0, tiled=True)
    grad_start = lax.all_gather(grad_start, "mp", axis=0, tiled=True)
    grads = lax.psum_scatter(grads, "dp", scatter_dimension=1, tiled=True)
    grads = lax.psum_scatter(grads, "mp", scatter_dimension=0).astype(jnp.float32)
    norm_share = lax.psum(
        lax.psum_scatter(grad_norm_rows, "dp", scatter_dimension=1, tiled=True), "mp"
    )
    edge = 4 * QKV
    shares = (
        jnp.stack([grads[:, :QKV], grads[:, QKV : 2 * QKV], grads[:, 2 * QKV : 3 * QKV]]),
        grads[:, 3 * QKV : edge].T,
        grads[:, edge : edge + HIDDEN],
        grads[:, edge + HIDDEN :].T,
        norm_share,
    )
    mp_count = lax.axis_size("mp")
    squares = jnp.sum(shares[4] * shares[4]) / mp_count
    for grad_part in shares[:4]:
        squares = squares + jnp.sum(grad_part * grad_part)
    grad_norm = jnp.sqrt(lax.psum(squares, ("dp", "mp")))
    factor = jnp.minimum(1.0, CLIP_AT / (grad_norm + 1e-06))
    norm_grad = shares[4] * factor
    qkv_new = adam_step(w_qkv, shares[0] * factor, qkv_first, qkv_second, RATE_MATRIX, WEIGHT_DECAY)
    out_new = adam_step(w_out, shares[1] * factor, out_first, out_second, RATE_OUT, WEIGHT_DECAY)
    up_new = adam_step(w_up, shares[2] * factor, up_first, up_second, RATE_MATRIX, WEIGHT_DECAY)
    down_new = adam_step(
        w_down, shares[3] * factor, down_first, down_second, RATE_MATRIX, WEIGHT_DECAY
    )
    norm_new = adam_step(norm_params, norm_grad, norm_first, norm_second, RATE_VECTOR, 0.0)
    return (
        result,
        grad_start,
        grad_norm,
        qkv_new[0],
        qkv_new[1],
        qkv_new[2],
        out_new[0],
        out_new[1],
        out_new[2],
        up_new[0],
        up_new[1],
        up_new[2],
        down_new[0],
        down_new[1],
        down_new[2],
        norm_new[0],
        norm_new[1],
        norm_new[2],
        norm_grad,
    )


def solution(mesh):
    return jax.shard_map(
        body,
        mesh=mesh,
        in_specs=(
            P("dp", None),
            P("dp", None),
            P("dp", None),
            P("dp", None),
            P(None, "dp", "mp"),
            P("mp", "dp"),
            P("dp", "mp"),
            P("mp", "dp"),
            P(None, "dp"),
            P(None, "dp", "mp"),
            P(None, "dp", "mp"),
            P("mp", "dp"),
            P("mp", "dp"),
            P("dp", "mp"),
            P("dp", "mp"),
            P("mp", "dp"),
            P("mp", "dp"),
            P(None, "dp"),
            P(None, "dp"),
        ),
        out_specs=(
            P("dp", None),
            P("dp", None),
            P(),
            P(None, "dp", "mp"),
            P(None, "dp", "mp"),
            P(None, "dp", "mp"),
            P("mp", "dp"),
            P("mp", "dp"),
            P("mp", "dp"),
            P("dp", "mp"),
            P("dp", "mp"),
            P("dp", "mp"),
            P("mp", "dp"),
            P("mp", "dp"),
            P("mp", "dp"),
            P(None, "dp"),
            P(None, "dp"),
            P(None, "dp"),
            P(None, "dp"),
        ),
        check_vma=False,
    )
```

time: 1220 us -> 644 us (0.53)
  waiting for transfers between devices: 740 us -> 168 us
  local copies, waits for them, and re-layouts: 35.5 us -> 105 us
  other arithmetic: 58.7 us -> 27.1 us
  blocking collectives: 264 us -> 239 us
  matrix products: 92.8 us -> 78.3 us
    psum x3 -> x0, waiting for transfers between devices: 355 us -> none  [the longest x1 127 us: micro_pass(): lax.psum(mlp_part.astype(jnp.bfloat16), 'mp').astype(jnp.float32)]
    reduce_scatter x6 -> x1, waiting for transfers between devices: 273 us -> 0.02 us  [body(): lax.psum_scatter(grads, 'mp', scatter_dimension=0).astype(jnp.float32)]
    all_gather x2 -> x3, waiting for transfers between devices: 0.03 us -> 38.2 us  [the longest x1 38.2 us: body(): weights = lax.all_gather(weights, 'dp', axis=1, tiled=True)]
    all_gather x3 -> x2, blocking collectives: 73.2 us -> 39.6 us  [the longest x1 26.6 us: body(): lax.all_gather(norm_params.astype(low), 'dp', axis=1, tiled=True)]
    slice x2 -> x7, local copies, waits for them, and re-layouts: 0.04 us -> 27.6 us  [the longest x2 12.1 us: layer_pass(): w_qkv = weights[:, :, :3 * QKV].reshape(blocks, model, 3, QKV)]
    concatenate x0 -> x2, local copies, waits for them, and re-layouts: none -> 22.7 us  [the longest x1 22.6 us: layer_pass(): grads = jnp.concatenate([grad_qkv, grad_out, grad_up, grad_down], axis=2)]
    unnamed x13 -> x6, waiting for transfers between devices: 113 us -> 130 us
    dot_general x36 -> x18, matrix products: 92.8 us -> 78.3 us  [the longest x1 20.3 us: layer_pass(): jnp.einsum('td,mdf->mtf', normed_two, w_up, preferred_element_type=jnp.fl...]
  transfers between devices with their start and end apart: 12 -> 5, of which waited for: 8 -> 2; matrix products, arithmetic and copies ran while one was open for 10% -> 4% of each run, Pallas kernels for 0% -> 0%
where the time goes in v1:
time: 644 us; the launch traced here: 639 us
  blocking collectives  239 us (37%)
  waiting for transfers between devices  168 us (26%)
  local copies, waits for them, and re-layouts  105 us (16%)
  matrix products  78.3 us (12%)
  other arithmetic  27.1 us (4%)
  between operations  20.5 us (3%)
    unnamed x6, waiting for transfers between devices  130 us
    unnamed x1, blocking collectives  122 us
    psum x1, blocking collectives, body(): grad_norm = jnp.sqrt(lax.psum(squares, ('dp', 'mp')))  68.9 us
    all_gather x1, waiting for transfers between devices, body(): weights = lax.all_gather(weights, 'dp', axis=1, tiled=True)  38.2 us
    all_gather x1, blocking collectives, body(): lax.all_gather(norm_params.astype(low), 'dp', axis=1, tiled=True)  26.6 us
    unnamed x127, local copies, waits for them, and re-layouts  26.1 us
    concatenate x1, local copies, waits for them, and re-layouts, layer_pass(): grads = jnp.concatenate([grad_qkv, grad_out, grad_up, grad_down], axis=2)  22.6 us
    dot_general x1, matrix products, layer_pass(): jnp.einsum('td,mdf->mtf', normed_two, w_up, preferred_element_type=jnp.fl...  20.3 us
  transfers between devices with their start and end apart: 5, of which 2 were waited for; matrix products, arithmetic and copies ran while one was open for 4% of the time, Pallas kernels for 0%

profile of v1, /device:TPU:1, one launch (start us, length us, event | category | flops | bytes accessed | tf_op | source)
XLA Modules:
  0.0 639.3 jit_solution(2522658802624226727)
XLA Ops:
  11.0 13.0 %all_gather.16 = bf16[4,24,2304]{2,1,0:T(8,128)(2,1)S(1)} all-gather(bf16[1,24,2304]{2,1,0:T(8,128)(2,1)S(1)} %concatenate.25), channel_id=1, replica_groups=mesh['dp'=32,'mp'=4] {'mp'}, dimensions={0}, use_global_device_ids=true | all-gather | bytes 552960 | tf_op jit(solution)/shard_map/all_gather | solution.py:206
  27.4 26.6 %all-gather = bf16[32,24,4]{1,2,0:T(4,128)(2,1)S(1)} all-gather(bf16[1,24,4]{1,2,0:T(4,128)(2,1)S(1)} %convert_bitcast_fusion.7), channel_id=1, replica_groups=mesh['dp'=32,'mp'=4] {'dp'}, dimensions={0}, use_global_device_ids=true | all-gather | bytes 6336 | tf_op jit(solution)/shard_map/all_gather | solution.py:208
  57.1 38.2 %all-gather.5.cloned.1.call-done = bf16[4,768,2304]{2,0,1:T(4,128)(2,1)} async-done(((bf16[4,24,2304]{2,0,1:T(4,128)(2,1)}), bf16[4,768,2304]{2,0,1:T(4,128)(2,1)}) %all-gather.5.cloned.1.call-update) | async-done | bytes 14155792 | tf_op jit(solution)/shard_map/all_gather | solution.py:207
  95.2 2.9 slice.97
  100.9 5.3 slice.91
  106.2 6.7 %copy.202 = bf16[4,768,576]{1,2,0:T(8,128)(2,1)S(1)} copy(bf16[4,768,576]{2,0,1:T(4,128)(2,1)} %slice.91) | data formatting | bytes 7077888 | tf_op jit(solution)/shard_map/slice | solution.py:70
  113.0 10.6 %fusion.96 = (bf16[4,768,768]{2,0,1:T(4,128)(2,1)}, bf16[4,768,768]{2,0,1:T(4,128)(2,1)}) fusion(bf16[4,768,2304]{2,0,1:T(4,128)(2,1)} %all-gather.5.cloned.1.call-done), kind=kLoop, calls=%fused_computation.179 | loop fusion | bytes 18874368 | tf_op jit(solution)/shard_map/slice | solution.py:73
  123.6 8.5 %copy.245 = bf16[4,768,768]{1,2,0:T(8,128)(2,1)} copy(bf16[4,768,768]{2,0,1:T(4,128)(2,1)} %get-tuple-element.90) | data formatting | bytes 9437184
  132.0 3.3 convert_bitcast_fusion.3
  155.9 20.3 %fusion.10 = (bf16[4,512,768]{1,2,0:T(8,128)(2,1)}, f32[4,512,768]{1,2,0:T(8,128)}, f32[4,768,512]{2,1,0:T(8,128)}) fusion(bf16[4,768,768]{1,2,0:T(8,128)(2,1)} %copy.245, f32[512,768]{1,0:T(8,128)S(1)} %get-tuple-element.104, f32[768]{0:T(1024)} %get-tuple-element.68, f32[768]{0:T(1024)S(1)} %copy-done.41, f32[512]{0:T(512)S(1)} %add_rsqrt_fusion, ...), kind=kOutput, calls=%fused_computation.19 | convolution fusion | flops 2520121344 | bytes 22030336 | tf_op jit(solution)/shard_map/td,mdf->mtf/dot_general | solution.py:107
  176.2 7.9 %fusion.7 = bf16[4,512,768]{1,2,0:T(8,128)(2,1)S(1)} fusion(f32[4,512,768]{1,2,0:T(8,128)} %get-tuple-element.88, f32[4,768,512]{2,1,0:T(8,128)} %get-tuple-element.105, bf16[4,768,768]{2,0,1:T(4,128)(2,1)S(1)} %bitcast.267, bf16[2048,768]{1,0:T(8,128)(2,1)S(1)} %copy-done.26, s32[]{:T(128)S(6)} %select_n.12), kind=kOutput, calls=%fused_computation.11 | convolution fusion | flops 2437939200 | bytes 21233668 | tf_op jit(solution)/shard_map/td,mdf->mtf/dot_general | solution.py:114
  184.1 3.7 fusion.33
  187.9 5.0 convert_bitcast_fusion.1
  200.1 3.4 fusion.47
  213.1 7.0 %convert_bitcast_fusion = bf16[4,768,768]{1,2,0:T(8,128)(2,1)} fusion(bf16[4,512,768]{1,2,0:T(8,128)(2,1)} %get-tuple-element.87, bf16[2048,768]{1,0:T(8,128)(2,1)} %param.22, s32[]{:T(128)S(6)} %select_n.12), kind=kOutput, calls=%fused_computation.33 | convolution fusion | flops 2418278400 | bytes 8650756 | tf_op jit(solution)/shard_map/td,mtf->mdf/dot_general | solution.py:113
  236.7 6.5 %pad_maximum_fusion = bf16[4,768,2304]{1,2,0:T(8,128)(2,1)} fusion(bf16[4,768,768]{1,2,0:T(8,128)(2,1)S(1)} %bitcast.263, bf16[4,768,768]{1,2,0:T(8,128)(2,1)S(1)} %bitcast.261, bf16[4,768,192]{1,2,0:T(8,128)(2,1)S(1)} %copy-done.9, bf16[4,768,576]{1,2,0:T(8,128)(2,1)S(1)} %bitcast.259), kind=kLoop, calls=%fused_computation.1 | loop fusion | flops 56623104 | bytes 28311552 | tf_op jit(solution)/shard_map/concatenate | solution.py:161
  243.1 22.6 %copy.230 = bf16[4,768,2304]{2,0,1:T(4,128)(2,1)} copy(bf16[4,768,2304]{1,2,0:T(8,128)(2,1)} %pad_maximum_fusion) | data formatting | bytes 28311552 | tf_op jit(solution)/shard_map/concatenate | solution.py:161
  265.8 7.3 %fusion.34 = bf16[512,768]{1,0:T(8,128)(2,1)} fusion(f32[512,768]{1,0:T(8,128)} %copy-done.4, bf16[4,512,768]{1,2,0:T(8,128)(2,1)} %get-tuple-element.87, bf16[4,768,768]{2,0,1:T(4,128)(2,1)} %get-tuple-element.89), kind=kOutput, calls=%fused_computation.57 | convolution fusion | flops 2416705536 | bytes 10223616 | tf_op jit(solution)/shard_map/mtf,mdf->td/dot_general | solution.py:110
  274.5 130.1 %all-reduce.4.cloned.1.call-done = bf16[4,768,2304]{2,0,1:T(4,128)(2,1)} async-done(((bf16[4,768,2304]{2,0,1:T(4,128)(2,1)}), bf16[4,768,2304]{2,0,1:T(4,128)(2,1)}) %all-reduce.4.cloned.1.call-update) | async-done | bytes 14155792
  406.6 5.2 fusion.32
  414.9 122.0 %all-reduce = f32[4,768]{1,0:T(4,128)S(1)} all-reduce(f32[4,768]{1,0:T(4,128)S(1)} %pad_maximum_fusion.2), channel_id=2, replica_groups=mesh['dp'=32,'mp'=4] {'dp'}, use_global_device_ids=true, to_apply=%region_15.16.clone | all-reduce | flops 3072 | bytes 24576
  537.0 8.9 %psum.14 = f32[4,24]{1,0:T(4,128)S(1)} all-reduce(f32[4,24]{1,0:T(4,128)S(1)} %constant_dynamic-slice_fusion.2), channel_id=1, replica_groups=mesh['dp'=32,'mp'=4] {'mp'}, use_global_device_ids=true, to_apply=%region_16.17 | all-reduce | flops 96 | bytes 768 | tf_op jit(solution)/shard_map/psum | solution.py:225
  552.7 68.9 %psum.15 = f32[]{:T(128)} all-reduce(f32[]{:T(128)S(6)} %add.177), channel_id=1, replica_groups=mesh['dp'=32,'mp'=4] {'dp','mp'}, use_global_device_ids=true, to_apply=%region_24.25 | all-reduce | flops 1 | bytes 8 | tf_op jit(solution)/shard_map/psum | solution.py:240
  625.8 3.9 copy.284
  (212 shorter events, 81.1 us)
Async XLA Ops:
  7.2 49.1 %copy-start = (s32[16,128]{1,0:T(8,128)S(1)}, s32[16,128]{1,0:T(8,128)}, u32[]{:S(2)}) copy-start(s32[16,128]{1,0:T(8,128)} %param.21) | copy-start | bytes 24580
  7.2 88.0 %all-gather.5.cloned.1.call-start = ((), (), s32[]{:S(2)}) async-start(), calls=%async_computation.1 | async-start | bytes 14598144 | tf_op jit(solution)/shard_map/all_gather | solution.py:207
  24.9 379.6 %all-reduce.4.cloned.1.call-start = ((), (), s32[]{:S(2)}) async-start(), calls=%async_computation.5 | async-start | bytes 28311552
  25.7 72.5 %copy-start.21 = (f32[4,768]{1,0:T(4,128)}, f32[4,768]{1,0:T(4,128)S(1)}, u32[]{:S(2)}) copy-start(f32[4,768]{1,0:T(4,128)S(1)} %dynamic-slice_convert_fusion) | copy-start | bytes 36868
  55.0 45.9 %copy-start.37 = (f32[512]{0:T(512)}, f32[512]{0:T(512)S(1)}, u32[]{:S(2)}) copy-start(f32[512]{0:T(512)S(1)} %add_rsqrt_fusion.1) | copy-start | bytes 6148
  265.8 140.8 %copy-start.38 = (f32[512]{0:T(512)S(1)}, f32[512]{0:T(512)}, u32[]{:S(2)}) copy-start(f32[512]{0:T(512)} %copy-done.37) | copy-start | bytes 6148
  265.8 281.4 %all-gather.7.cloned.1.call-start = ((), (), s32[]{:S(2)}) async-start(), calls=%async_computation.2 | async-start | bytes 3932160 | tf_op jit(solution)/shard_map/all_gather | solution.py:221
  273.1 274.1 %reduce-scatter.3.cloned.1.call-start = ((), (), s32[]{:S(2)}) async-start(), calls=%async_computation.4 | async-start | bytes 552960 | tf_op jit(solution)/shard_map/reduce_scatter | solution.py:224
  406.5 146.1 %all-gather.9.cloned.1.call-start = ((), (), s32[]{:S(2)}) async-start(), calls=%async_computation.3 | async-start | bytes 3932160 | tf_op jit(solution)/shard_map/all_gather | solution.py:222
  411.8 210.5 %copy-start.44 = (f32[4,24]{1,0:T(4,128)S(1)}, f32[4,24]{1,0:T(4,128)}, u32[]{:S(2)}) copy-start(f32[4,24]{1,0:T(4,128)} %param.27) | copy-start | bytes 1156
  411.8 210.5 %copy-start.48 = (f32[4,24]{1,0:T(4,128)S(1)}, f32[4,24]{1,0:T(4,128)}, u32[]{:S(2)}) copy-start(f32[4,24]{1,0:T(4,128)} %param.37) | copy-start | bytes 1156
  411.8 210.5 %copy-start.49 = (f32[4,24]{1,0:T(4,128)S(1)}, f32[4,24]{1,0:T(4,128)}, u32[]{:S(2)}) copy-start(f32[4,24]{1,0:T(4,128)} %param.36) | copy-start | bytes 1156
  411.8 211.1 %copy-start.27 = (f32[192,24]{0,1:T(8,128)S(1)}, f32[192,24]{0,1:T(8,128)}, u32[]{:S(2)}) copy-start(f32[192,24]{0,1:T(8,128)} %param.24) | copy-start | bytes 55300
  411.8 211.1 %copy-start.39 = (f32[192,24]{0,1:T(8,128)S(1)}, f32[192,24]{0,1:T(8,128)}, u32[]{:S(2)}) copy-start(f32[192,24]{0,1:T(8,128)} %param.31) | copy-start | bytes 55300
  411.9 211.1 %copy-start.40 = (f32[192,24]{0,1:T(8,128)S(1)}, f32[192,24]{0,1:T(8,128)}, u32[]{:S(2)}) copy-start(f32[192,24]{0,1:T(8,128)} %param.30) | copy-start | bytes 55300
  411.9 211.8 %copy-start.23 = (f32[3,24,192]{2,1,0:T(8,128)S(1)}, f32[3,24,192]{2,1,0:T(8,128)}, u32[]{:S(2)}) copy-start(f32[3,24,192]{2,1,0:T(8,128)} %param.23) | copy-start | bytes 165892
  411.9 211.8 %copy-start.28 = (f32[3,24,192]{2,1,0:T(8,128)S(1)}, f32[3,24,192]{2,1,0:T(8,128)}, u32[]{:S(2)}) copy-start(f32[3,24,192]{2,1,0:T(8,128)} %param.29) | copy-start | bytes 165892
  411.9 211.8 %copy-start.29 = (f32[3,24,192]{2,1,0:T(8,128)S(1)}, f32[3,24,192]{2,1,0:T(8,128)}, u32[]{:S(2)}) copy-start(f32[3,24,192]{2,1,0:T(8,128)} %param.28) | copy-start | bytes 165892
  411.9 212.5 %copy-start.24 = (f32[768,24]{0,1:T(8,128)S(1)}, f32[768,24]{0,1:T(8,128)}, u32[]{:S(2)}) copy-start(f32[768,24]{0,1:T(8,128)} %param.26) | copy-start | bytes 221188
  411.9 212.5 %copy-start.30 = (f32[768,24]{0,1:T(8,128)S(1)}, f32[768,24]{0,1:T(8,128)}, u32[]{:S(2)}) copy-start(f32[768,24]{0,1:T(8,128)} %param.35) | copy-start | bytes 221188
  411.9 212.5 %copy-start.31 = (f32[768,24]{0,1:T(8,128)S(1)}, f32[768,24]{0,1:T(8,128)}, u32[]{:S(2)}) copy-start(f32[768,24]{0,1:T(8,128)} %param.34) | copy-start | bytes 221188
  411.9 213.2 %copy-start.25 = (f32[24,768]{1,0:T(8,128)S(1)}, f32[24,768]{1,0:T(8,128)}, u32[]{:S(2)}) copy-start(f32[24,768]{1,0:T(8,128)} %param.25) | copy-start | bytes 221188
  412.0 213.2 %copy-start.32 = (f32[24,768]{1,0:T(8,128)S(1)}, f32[24,768]{1,0:T(8,128)}, u32[]{:S(2)}) copy-start(f32[24,768]{1,0:T(8,128)} %param.33) | copy-start | bytes 221188
  412.0 213.1 %copy-start.33 = (f32[24,768]{1,0:T(8,128)S(1)}, f32[24,768]{1,0:T(8,128)}, u32[]{:S(2)}) copy-start(f32[24,768]{1,0:T(8,128)} %param.32) | copy-start | bytes 221188
  (40 other events, 306.1 us)
Sparse Core Ops, SparseCore 0:
  25.0 70.1 all-gather.4
  265.9 138.5 all-reduce.3
  406.3 39.6 all-gather.6
  448.4 19.2 reduce-scatter.2
  469.8 41.4 all-gather.8

commit v2 on v0

v2 whole, which is shorter than its diff:
```python
import jax
import jax.numpy as jnp
from jax import lax
from jax.experimental import pallas as pl
from jax.experimental.pallas import tpu as pltpu
from jax.sharding import PartitionSpec as P

MESH = pl.DeviceIdType.MESH

BF = jnp.bfloat16
F32 = jnp.float32
HEAD = 64
LEN = 128
ROWS = 512
D = 768
SEQS = 4
WIDE = 384
CLIP_AT = 1.0
BETA_ONE = 0.9
BETA_TWO = 0.95
ADAM_EPS = 1e-08
STEP = 10
WEIGHT_DECAY = 0.01
RATE_MATRIX = 0.05
RATE_OUT = 0.3
RATE_VECTOR = 0.5
COPIES = 320
NORM_EPS = 1e-05


def nn(a, b):
    return jnp.dot(a, b, preferred_element_type=F32)


def nt(a, b):
    return lax.dot_general(a, b, (((1,), (1,)), ((), ())), preferred_element_type=F32)


def tn(a, b):
    return lax.dot_general(a, b, (((0,), (0,)), ((), ())), preferred_element_type=F32)


def whole(W, p, owner, zp):
    return W[p, owner, zp].reshape(D, D)


def columns(W, zp, base):
    return W[0, 1, zp, :, :, :, base : base + 256].reshape(D, 256)


def tiles(x):
    return x.astype(BF).reshape(4, 4, 48, x.shape[1])


def norm_stats(x):
    center = jnp.mean(x, axis=-1, keepdims=True)
    off = x - center
    inv = lax.rsqrt(jnp.mean(off * off, axis=-1, keepdims=True) + NORM_EPS)
    return off * inv, inv


def low_lanes(x):
    lane = lax.broadcasted_iota(jnp.int32, x.shape, x.ndim - 1)
    return lane < HEAD


def split_heads(x):
    first = low_lanes(x)
    zero = jnp.zeros_like(x)
    return jnp.concatenate([jnp.where(first, x, zero), jnp.where(first, zero, x)], axis=0)


def swap_halves(x):
    return pltpu.roll(x.astype(F32), HEAD, 1).astype(x.dtype)


def seq_rows(s):
    return pl.ds(pl.multiple_of(s * LEN, LEN), LEN)


def first_norm(place, tok, time, gains, segs, xs, n1, bias):
    for s in range(SEQS):
        rows = slice(s * LEN, s * LEN + LEN)
        x = tok[rows, :].astype(F32) + time[pl.ds(SEQS * place + s, 1), :]
        xs[rows, :] = x
        scaled, _ = norm_stats(x)
        n1[rows, :] = (scaled * gains[0:1, :] + gains[1:2, :]).astype(BF)
        lab = jnp.broadcast_to(segs[pl.ds(SEQS * place + s, 1), :].astype(F32), (LEN, LEN))
        bias[s] = jnp.where(lab == lab.T, 0.0, -1e30).astype(F32)


def project(n1, W, pq, pv):
    for zp in range(2):
        pq[zp] = nn(n1[...], whole(W, 0, 0, zp)).astype(BF)
        for j in range(2):
            pv[2 * zp + j] = nn(n1[...], columns(W, zp, 384 * j)).astype(BF)


def softmax_rows(scores):
    e = jnp.exp(scores - jnp.max(scores, axis=-1, keepdims=True))
    return e / jnp.sum(e, axis=-1, keepdims=True)


def value_two(vg):
    first = low_lanes(vg)
    return swap_halves(jnp.where(first, vg, jnp.zeros_like(vg)))


def attention(lo, hi, pq, pv, bias, probs, mx):
    scaling = HEAD ** (-0.5)

    def step(i, _):
        s, zp = i // 2, i % 2
        rows = seq_rows(s)
        mask = bias[s]
        mask2 = jnp.concatenate([mask, mask], axis=0)
        for j in range(2):
            z = 2 * zp + j
            base = 384 * j
            ga = pq[zp, rows, base : base + 128]
            gb = pq[zp, rows, base + 128 : base + 256]
            gc = pq[zp, rows, base + 256 : base + 384]
            va = pv[z, rows, 0:128]
            vb = value_two(pv[z, rows, 128:256])
            p01 = softmax_rows(nt(split_heads(ga), gc) * scaling + mask2).astype(BF)
            first = low_lanes(gb)
            p2 = softmax_rows(
                nt(jnp.where(first, gb, jnp.zeros_like(gb)), swap_halves(gb)) * scaling + mask
            ).astype(BF)
            probs[s, z, 0:256, :] = p01
            probs[s, z, 256:384, :] = p2
            m01 = nn(jnp.concatenate([p01[:LEN], p01[LEN:]], axis=1), split_heads(va))
            mx[z, rows, 128:256] = m01.astype(BF)
            mx[z, rows, 0:128] = nn(p2, vb).astype(BF)
        return 0

    lax.fori_loop(lo, hi, step, 0)


def second_norm(W, mx, xs, gains, mid, n2):
    acc = xs[...]
    for z in range(4):
        base = 384 * (z % 2) + 128
        acc = acc + nt(mx[z], columns(W, z // 2, base))
    mid[...] = acc

    def per_seq(s, _):
        rows = seq_rows(s)
        scaled, _ = norm_stats(mid[rows, :])
        n2[rows, :] = (scaled * gains[2:3, :] + gains[3:4, :]).astype(BF)
        return 0

    lax.fori_loop(0, SEQS, per_seq, 0)


def gelu_parts(u):
    cdf = 0.5 * (1.0 + lax.erf(u * 0.7071067811865476))
    pdf = jnp.exp(u * u * -0.5) * 0.3989422804014327
    return u * cdf, cdf + u * pdf


def feed_forward(p, zp, W, G, n2, ct, act, gbef, acc_out, acc_g, first):
    for h in range(2):
        rows = slice(256 * h, 256 * h + 256)
        a, slope = gelu_parts(nn(n2[rows, :], whole(W, p, 0, zp)))
        act[rows, :] = a.astype(BF)
        gbef[rows, :] = (nn(ct[rows, :], whole(W, p, 1, zp)) * slope).astype(BF)
    out = nt(act[...], whole(W, p, 1, zp))
    back = nt(gbef[...], whole(W, p, 0, zp))
    if first:
        acc_out[...] = out
        acc_g[...] = back
    else:
        acc_out[...] += out
        acc_g[...] += back
    G[p, 1, zp] = tiles(tn(ct[...], act[...]))
    G[p, 0, zp] = tiles(tn(n2[...], gbef[...]))


def norm_back(grad, scaled, inv, gain):
    u = grad * gain
    m1 = jnp.mean(u, axis=-1, keepdims=True)
    m2 = jnp.mean(u * scaled, axis=-1, keepdims=True)
    return inv * (u - m1 - scaled * m2)


def second_back(mid, acc_g, ct, gains, br, ng):
    ng[...] = jnp.zeros_like(ng)

    def per_seq(s, _):
        rows = seq_rows(s)
        scaled, inv = norm_stats(mid[rows, :])
        g = acc_g[rows, :]
        ng[2:3, :] += jnp.sum(g * scaled, axis=0, keepdims=True)
        ng[3:4, :] += jnp.sum(g, axis=0, keepdims=True)
        gm = ct[rows, :].astype(F32) + norm_back(g, scaled, inv, gains[2:3, :])
        mid[rows, :] = gm
        br[rows, :] = gm.astype(BF)
        return 0

    lax.fori_loop(0, SEQS, per_seq, 0)


def mixed_grad(W, br, dm):
    for z in range(4):
        base = 384 * (z % 2) + 128
        dm[z] = nn(br[...], columns(W, z // 2, base)).astype(BF)


def attention_back(lo, hi, pq, pv, probs, dm, dpq, dpv):
    scaling = HEAD ** (-0.5)

    def step(i, _):
        s, zp = i // 2, i % 2
        rows = seq_rows(s)
        for j in range(2):
            z = 2 * zp + j
            base = 384 * j
            ga = pq[zp, rows, base : base + 128]
            gb = pq[zp, rows, base + 128 : base + 256]
            gc = pq[zp, rows, base + 256 : base + 384]
            va = pv[z, rows, 0:128]
            vb = value_two(pv[z, rows, 128:256])
            p01 = probs[s, z, 0:256, :]
            p2 = probs[s, z, 256:384, :]
            db = dm[z, rows, 0:128]
            da = split_heads(dm[z, rows, 128:256])
            gp = nt(da, va)
            pf = p01.astype(F32)
            ds01 = (pf * (gp - jnp.sum(gp * pf, axis=-1, keepdims=True))).astype(BF)
            gp2 = nt(db, vb)
            pf2 = p2.astype(F32)
            ds2 = (pf2 * (gp2 - jnp.sum(gp2 * pf2, axis=-1, keepdims=True))).astype(BF)
            dv01 = tn(p01, da)
            dv2 = pltpu.roll(tn(p2, db), HEAD, 1)
            dk01 = tn(ds01, split_heads(ga)) * scaling
            dq01 = nn(jnp.concatenate([ds01[:LEN], ds01[LEN:]], axis=1), split_heads(gc)) * scaling
            both = swap_halves(gb)
            dq2 = nn(ds2, both)
            dk2 = tn(ds2, both)
            first = low_lanes(dq2)
            dpq[zp, rows, base : base + 128] = dq01.astype(BF)
            dpq[zp, rows, base + 128 : base + 256] = (jnp.where(first, dq2, dk2) * scaling).astype(BF)
            dpq[zp, rows, base + 256 : base + 384] = dk01.astype(BF)
            dpv[z, rows, 0:128] = dv01.astype(BF)
            dpv[z, rows, 128:256] = jnp.where(first, dv2, 0.0).astype(BF)
        return 0

    lax.fori_loop(lo, hi, step, 0)


def input_grad_sum(W, dpq, dpv, gn):
    acc = nt(dpq[0], whole(W, 0, 0, 0)) + nt(dpq[1], whole(W, 0, 0, 1))
    for z in range(4):
        acc = acc + nt(dpv[z], columns(W, z // 2, 384 * (z % 2)))
    gn[...] = acc


def first_grads(zp, G, n1, br, mx, dpq, dpv):
    G[0, 0, zp] = tiles(tn(n1[...], dpq[zp]))
    for j in range(2):
        z = 2 * zp + j
        base = 384 * j
        gv = tn(n1[...], dpv[z])
        go = tn(br[...], mx[z])
        G[0, 1, zp, :, :, :, base : base + 128] = tiles(gv[:, :128])
        G[0, 1, zp, :, :, :, base + 128 : base + 256] = tiles(gv[:, 128:] + go[:, :128])
        G[0, 1, zp, :, :, :, base + 256 : base + 384] = tiles(go[:, 128:])


def first_back(xs, gn, mid, gains, ng, dx):
    def per_seq(s, _):
        rows = seq_rows(s)
        scaled, inv = norm_stats(xs[rows, :])
        g = gn[rows, :]
        ng[0:1, :] += jnp.sum(g * scaled, axis=0, keepdims=True)
        ng[1:2, :] += jnp.sum(g, axis=0, keepdims=True)
        dx[rows, :] = (mid[rows, :] + norm_back(g, scaled, inv, gains[0:1, :])).astype(BF)
        return 0

    lax.fori_loop(0, SEQS, per_seq, 0)


class Place:
    def __init__(self):
        dp = lax.axis_index("dp")
        self.dp = dp
        self.at = {"z": lax.axis_index("mp"), "y": dp // 8, "x": (dp // 2) % 4, "c": dp % 2}

    def step(self, axis, d):
        return (self.at[axis] + d) % (2 if axis == "c" else 4)

    def device(self, axis, d):
        q = dict(self.at)
        q[axis] = self.step(axis, d)
        return ((q["y"] * 4 + q["x"]) * 2 + q["c"], q["z"])


class Net:
    def __init__(self, place, send_sem, recv_sem):
        self.place, self.send_sem, self.recv_sem = place, send_sem, recv_sem
        self.count = 0
        self.sent = []

    def push(self, src, dst, axis, d, land):
        k = self.count
        self.count += 1
        to = self.place.device(axis, d)

        def copy(target):
            return pltpu.make_async_remote_copy(
                src_ref=src,
                dst_ref=target,
                send_sem=self.send_sem.at[k],
                recv_sem=self.recv_sem.at[k],
                device_id=to,
                device_id_type=MESH,
            )

        out = copy(dst)
        out.start()
        self.sent.append(out)
        return copy(land)

    def finish(self):
        for out in self.sent:
            out.wait_send()


def arrive(copies):
    for copy in copies:
        copy.wait_recv()


def lanes(z):
    return pl.ds(pl.multiple_of((z % 2) * WIDE, 128), WIDE)


def weight_view(W, p, owner, r, at):
    y = slice(None) if at["y"] is None else at["y"]
    x = slice(None) if at["x"] is None else at["x"]
    rows = pl.ds(16 * r, 16)
    if at["z"] is None:
        return W.at[p, owner, :, y, x, rows, :]
    return W.at[p, owner, at["z"] // 2, y, x, rows, lanes(at["z"])]


ORDERS = (("x", "y", "z"), ("y", "z", "x"), ("z", "x", "y"))


class Gather:
    def __init__(self, net, W, p):
        self.net, self.W, self.p = net, W, p
        self.core = net.place.at["c"]
        self.across = []
        self.waits = {}

    def view(self, r, at, owner=None):
        return weight_view(self.W, self.p, self.core if owner is None else owner, r, at)

    def known(self, r, done, **moved):
        at = dict(self.net.place.at)
        for axis in ORDERS[r][:done]:
            at[axis] = None
        at.update(moved)
        return at

    def spread(self, r, done, ds):
        axis = ORDERS[r][done]
        src = self.view(r, self.known(r, done))
        return [
            self.net.push(
                src, src, axis, d, self.view(r, self.known(r, done, **{axis: self.net.place.step(axis, -d)}))
            )
            for d in ds
        ]

    def share(self, r, at):
        src = self.view(r, at)
        self.across.append(self.net.push(src, src, "c", 1, self.view(r, at, 1 - self.core)))

    def first(self):
        for r in range(3):
            self.waits[r] = self.spread(r, 0, (1, 3, 2))

    def second(self):
        for r in range(3):
            arrive(self.waits[r])
            self.waits[r] = self.spread(r, 1, (1, 3, 2))

    def third(self):
        for r in range(3):
            arrive(self.waits[r])
            self.waits[r] = self.spread(r, 2, (1, 3))
        for r in range(3):
            self.share(r, self.known(r, 2))

    def half(self, r, d, side):
        axis = ORDERS[r][2]
        cut = "x" if axis == "y" else "y"
        return self.known(r, 2, **{axis: self.net.place.step(axis, d), cut: pl.ds(2 * side, 2)})

    def fourth(self):
        for r in range(3):
            axis = ORDERS[r][2]
            waits = []
            for side, d in ((0, 1), (1, 3)):
                self.waits[r][side].wait_recv()
                src = self.view(r, self.half(r, -d, side))
                waits.append(self.net.push(src, src, axis, d, self.view(r, self.half(r, 2, side))))
            self.waits[r] = waits
        for r in range(3):
            axis = ORDERS[r][2]
            for d in (3, 1):
                self.share(r, self.known(r, 2, **{axis: self.net.place.step(axis, d)}))

    def fifth(self):
        for r in range(3):
            axis = ORDERS[r][2]
            arrive(self.waits[r])
            self.share(r, self.known(r, 2, **{axis: self.net.place.step(axis, 2)}))

    def last(self):
        arrive(self.across)


class Scatter:
    def __init__(self, net, G, p, zp, slot, cross, half, full, small):
        self.net, self.G, self.p, self.zp, self.slot = net, G, p, zp, slot
        self.cross, self.half, self.full, self.small = cross, half, full, small
        self.core = net.place.at["c"]

    def view(self, j, y, x):
        return (self.p, self.core, self.zp, y, x, slice(None), pl.ds(WIDE * j, WIDE))

    def block(self, j, d, cut=slice(None)):
        if j == 0:
            return self.view(0, cut, self.net.place.step("x", d))
        return self.view(1, self.net.place.step("y", d), cut)

    def own(self, j, d):
        at = self.net.place.at
        if j == 0:
            return self.view(0, self.net.place.step("y", d), at["x"])
        return self.view(1, at["y"], self.net.place.step("x", d))

    def to_core(self):
        src = self.G.at[self.p, 1 - self.core, self.zp]
        self.waits = [self.net.push(src, self.cross.at[self.slot], "c", 1, self.cross.at[self.slot])]

    def add_core(self):
        arrive(self.waits)

        def per_y(y, _):
            at = (self.p, self.core, self.zp, y)
            self.G[at] = self.G[at] + self.cross[self.slot, y]
            return 0

        lax.fori_loop(0, 4, per_y, 0)
        self.waits = []
        for j, axis in ((0, "x"), (1, "y")):
            for side, d in ((0, 1), (1, 3)):
                src = self.G.at[self.block(j, 2, pl.ds(2 * side, 2))]
                dst = self.half.at[self.p, self.zp, j, side]
                self.waits.append((j, axis, side, d, self.net.push(src, dst, axis, d, dst)))

    def add_half(self):
        waits, self.waits = self.waits, []
        for j, axis, side, d, copy in waits:
            copy.wait_recv()
            at = self.block(j, d, pl.ds(2 * side, 2))
            self.G[at] = self.G[at] + self.half[self.p, self.zp, j, side]
            dst = self.full.at[self.p, self.zp, j, side]
            self.waits.append(self.net.push(self.G.at[self.block(j, d)], dst, axis, d, dst))

    def add_full(self):
        arrive(self.waits)
        self.waits = []
        for j, axis in ((0, "y"), (1, "x")):
            at = self.block(j, 0)
            total = self.G[at].astype(F32)
            for side in range(2):
                total = total + self.full[self.p, self.zp, j, side].astype(F32)
            self.G[at] = total.astype(BF)
            for d in (1, 3, 2):
                dst = self.small.at[self.p, self.zp, j, d - 1]
                self.waits.append(self.net.push(self.G.at[self.own(j, d)], dst, axis, d, dst))

    def add_small(self):
        arrive(self.waits)
        for j in range(2):
            at = self.own(j, 0)
            total = self.G[at].astype(F32)
            for d in range(3):
                total = total + self.small[self.p, self.zp, j, d].astype(F32)
            self.G[at] = total.astype(BF)


class Deep:
    def __init__(self, net, G, p, tiny, done):
        self.net, self.G, self.p, self.tiny, self.done = net, G, p, tiny, done

    def chunk(self, d):
        at = self.net.place.at
        z = self.net.place.step("z", d)
        return (self.p, at["c"], z // 2, at["y"], at["x"], slice(None), lanes(z))

    def send(self):
        self.waits = []
        for d in (1, 3, 2):
            dst = self.tiny.at[self.p, d - 1]
            self.waits.append(self.net.push(self.G.at[self.chunk(d)], dst, "z", d, dst))

    def add(self):
        arrive(self.waits)
        total = self.G[self.chunk(0)].astype(F32)
        for d in range(3):
            total = total + self.tiny[self.p, d].astype(F32)
        self.done[self.p] = total
        return jnp.sum(total * total)


class Sum:
    def __init__(self, net, slots):
        self.net, self.slots = net, slots

    def send(self, axis, value):
        slots = self.slots[axis]
        here = self.net.place.at[axis]
        self.axis = axis
        slots[here] = value
        self.waits = [
            self.net.push(slots.at[here], slots.at[here], axis, d, slots.at[self.net.place.step(axis, -d)])
            for d in ((1,) if axis == "c" else (1, 3, 2))
        ]

    def add(self):
        arrive(self.waits)
        slots = self.slots[self.axis]
        total = slots[0]
        for k in range(1, slots.shape[0]):
            total = total + slots[k]
        return total


class Rows:
    def __init__(self, net, rows_ref, out, sem):
        self.net, self.rows_ref, self.out, self.sem = net, rows_ref, out, sem

    def place_of(self, d, piece, side=None):
        start = ROWS * self.net.place.step("z", d) + 256 * piece
        if side is None:
            return self.out.at[pl.ds(pl.multiple_of(start, 256), 256), :]
        return self.out.at[pl.ds(pl.multiple_of(start + 128 * side, 128), 128), :]

    def send(self):
        start = pl.multiple_of(ROWS * self.net.place.at["z"], ROWS)
        self.local = pltpu.make_async_copy(self.rows_ref, self.out.at[pl.ds(start, ROWS), :], self.sem)
        self.local.start()
        self.near = []
        self.far = []
        for piece in range(2):
            src = self.rows_ref.at[pl.ds(256 * piece, 256), :]
            self.near.append(
                [self.net.push(src, self.place_of(0, piece), "z", d, self.place_of(-d, piece)) for d in (1, 3)]
            )

    def forward(self, piece):
        for side, d in ((0, 1), (1, 3)):
            self.near[piece][side].wait_recv()
            src = self.place_of(-d, piece, side)
            self.far.append(self.net.push(src, src, "z", d, self.place_of(2, piece, side)))

    def finish(self):
        arrive(self.far)
        self.local.wait()


def pack(wq, wo, wu, wd, keep):
    q, k, v, o = wq[0], wq[1], wq[2], wo[...]
    keep[0, 0] = jnp.concatenate([q, k[:, 128:], k[:, :128]], axis=1)
    keep[1, 0] = jnp.concatenate([v, o[:, 128:], o[:, :128]], axis=1)
    for half in range(2):
        keep[0, 1 + half] = wu[:, WIDE * half : WIDE * half + WIDE]
        keep[1, 1 + half] = wd[:, WIDE * half : WIDE * half + WIDE]


def layer_kernel(
    tokens, time_emb, segs, cotangent, wq, wo, wu, wd, norm,
    out, input_grad, shards, norm_sum, square_sum,
    W, G, cross, half, full, small, tiny, done, keep, other,
    gx, gy, gc, nx, ny, nz, nc, sx, sy, sz, sc, gains, time, ng,
    xs, n1, bias, pq, pv, probs, mx, mid, n2, act, gbef, acc_out, acc_g, dm, dpq, dpv, tok, ct,
    send_sem, recv_sem, local_sem, free_sem,
):
    place = Place()
    net = Net(place, send_sem, recv_sem)
    z, core = place.at["z"], place.at["c"]
    mine = pl.ds(pl.multiple_of(ROWS * z, ROWS), ROWS)
    loads = [
        pltpu.make_async_copy(tokens.at[mine, :], tok, local_sem.at[0]),
        pltpu.make_async_copy(cotangent.at[mine, :], ct, local_sem.at[1]),
    ]
    for load in loads:
        load.start()
    barrier = pltpu.get_barrier_semaphore()
    for axis in ("x", "y", "z"):
        for d in (1, 2, 3):
            pl.semaphore_signal(barrier, inc=1, device_id=place.device(axis, d), device_id_type=MESH)
    pl.semaphore_signal(barrier, inc=1, device_id=place.device("c", 1), device_id_type=MESH)
    pack(wq, wo, wu, wd, keep)
    time[...] = time_emb[...].astype(F32)
    column = lax.broadcasted_iota(jnp.int32, (24, D), 1)
    row = lax.broadcasted_iota(jnp.int32, (24, D), 0)
    spot = jnp.where(column == row + 24 * place.dp, 1.0, 0.0).astype(F32)
    rounded = norm[...].astype(BF).astype(F32)
    spread = jnp.concatenate([nn(rounded, spot), jnp.zeros((4, D), F32)], axis=0)
    pl.semaphore_wait(barrier, 10)

    swap = net.push(keep.at[1 - core], other, "c", 1, other)
    gain_sum = Sum(net, {"x": gx, "y": gy, "c": gc})
    gain_sum.send("x", spread)
    swap.wait_recv()
    for p in range(3):
        kept = keep[core, p]
        came = other[p]
        even = core == 0
        rows = jnp.concatenate([jnp.where(even, kept, came), jnp.where(even, came, kept)], axis=0)
        W[p, core, z // 2, place.at["y"], place.at["x"], :, lanes(z)] = rows.astype(BF)
    parts = [Gather(net, W, p) for p in range(3)]
    for part in parts:
        part.first()
    gain_sum.send("y", gain_sum.add())
    for part in parts:
        part.second()
    gain_sum.send("c", gain_sum.add())
    parts[0].third()
    parts[1].third()
    gains[...] = gain_sum.add()
    for load in loads:
        load.wait()
    first_norm(z, tok, time, gains, segs, xs, n1, bias)
    parts[0].fourth()
    parts[2].third()
    parts[0].fifth()
    parts[0].last()

    project(n1, W, pq, pv)
    parts[1].fourth()
    attention(0, 4, pq, pv, bias, probs, mx)
    parts[1].fifth()
    parts[2].fourth()
    attention(4, 8, pq, pv, bias, probs, mx)
    second_norm(W, mx, xs, gains, mid, n2)
    parts[1].last()

    sums = {}
    for p, zp in ((1, 0), (1, 1), (2, 0), (2, 1), (0, 0), (0, 1)):
        sums[p, zp] = Scatter(net, G, p, zp, 2 * max(p - 1, 0) + zp, cross, half, full, small)
    deep = [Deep(net, G, p, tiny, done) for p in range(3)]

    def feed(p, zp):
        feed_forward(p, zp, W, G, n2, ct, act, gbef, acc_out, acc_g, p == 1 and zp == 0)
        sums[p, zp].to_core()

    def free():
        pl.semaphore_signal(free_sem, inc=1, device_id=place.device("c", 1), device_id_type=MESH)

    feed(1, 0)
    parts[2].fifth()
    feed(1, 1)
    sums[1, 0].add_core()
    free()
    parts[2].last()
    feed(2, 0)
    sums[1, 1].add_core()
    free()
    sums[1, 0].add_half()
    feed(2, 1)
    sums[2, 0].add_core()
    tok[...] = (mid[...] + acc_out[...]).astype(BF)
    out_rows = Rows(net, tok, out, local_sem.at[2])
    out_rows.send()
    sums[1, 1].add_half()
    sums[1, 0].add_full()
    second_back(mid, acc_g, ct, gains, act, ng)
    br = act
    sums[2, 1].add_core()
    sums[2, 0].add_half()
    sums[1, 1].add_full()
    mixed_grad(W, br, dm)
    sums[1, 0].add_small()
    attention_back(0, 4, pq, pv, probs, dm, dpq, dpv)
    sums[2, 1].add_half()
    sums[2, 0].add_full()
    sums[1, 1].add_small()
    deep[1].send()
    out_rows.forward(0)
    attention_back(4, 8, pq, pv, probs, dm, dpq, dpv)
    sums[2, 1].add_full()
    sums[2, 0].add_small()
    out_rows.forward(1)
    input_grad_sum(W, dpq, dpv, acc_g)
    first_back(xs, acc_g, mid, gains, ng, n2)
    in_rows = Rows(net, n2, input_grad, local_sem.at[3])
    in_rows.send()
    norm_total = Sum(net, {"c": nc, "x": nx, "y": ny, "z": nz})
    norm_total.send("c", ng[...])
    pl.semaphore_wait(free_sem, 2)
    first_grads(0, G, n1, br, mx, dpq, dpv)
    sums[0, 0].to_core()
    sums[2, 1].add_small()
    deep[2].send()
    first_grads(1, G, n1, br, mx, dpq, dpv)
    sums[0, 1].to_core()
    norm_total.send("x", norm_total.add())
    sums[0, 0].add_core()
    sums[0, 1].add_core()
    squares = deep[1].add() + deep[2].add()
    norm_total.send("y", norm_total.add())
    sums[0, 0].add_half()
    sums[0, 1].add_half()
    norm_total.send("z", norm_total.add())
    sums[0, 0].add_full()
    sums[0, 1].add_full()
    in_rows.forward(0)
    in_rows.forward(1)
    sums[0, 0].add_small()
    sums[0, 1].add_small()
    deep[0].send()
    norm_rows = norm_total.add()
    norm_sum[...] = norm_rows
    squares = squares + deep[0].add()
    other_rows = pl.ds(pl.multiple_of(24 * (1 - core), 8), 24)
    own_rows = pl.ds(pl.multiple_of(24 * core, 8), 24)
    trade = net.push(done.at[:, other_rows, :], shards.at[core], "c", 1, shards.at[1 - core])
    shards[core] = done[:, own_rows, :]
    total = Sum(net, {"c": sc, "x": sx, "y": sy, "z": sz})
    total.send("c", jnp.full((8, 128), squares, F32))
    total.send("x", total.add())
    total.send("y", total.add())
    total.send("z", total.add())
    square_sum[...] = total.add() + jnp.sum(norm_rows * norm_rows)
    trade.wait_recv()
    out_rows.finish()
    in_rows.finish()
    net.finish()


def layer(tokens, time_emb, segs, cotangent, wq, wo, wu, wd, norm):
    V = pltpu.VMEM
    rows, low = (ROWS, D), BF
    anywhere = pl.BlockSpec(memory_space=pl.ANY)
    near = pl.BlockSpec(memory_space=pltpu.VMEM)
    return pl.pallas_call(
        layer_kernel,
        name="layer",
        out_shape=(
            jax.ShapeDtypeStruct(tokens.shape, BF),
            jax.ShapeDtypeStruct(tokens.shape, BF),
            jax.ShapeDtypeStruct((2, 3, 24, WIDE), F32),
            jax.ShapeDtypeStruct((8, D), F32),
            jax.ShapeDtypeStruct((8, 128), F32),
        ),
        in_specs=[anywhere, near, near, anywhere] + [near] * 5,
        out_specs=[anywhere, anywhere, near, near, near],
        scratch_shapes=[
            V((3, 2, 2, 4, 4, 48, D), low),
            V((3, 2, 2, 4, 4, 48, D), low),
            V((4, 4, 4, 48, D), low),
            V((3, 2, 2, 2, 2, 48, WIDE), low),
            V((3, 2, 2, 2, 4, 48, WIDE), low),
            V((3, 2, 2, 3, 48, WIDE), low),
            V((3, 3, 48, WIDE), low),
            V((3, 48, WIDE), F32),
            V((2, 3, 24, WIDE), F32),
            V((3, 24, WIDE), F32),
            V((4, 8, D), F32),
            V((4, 8, D), F32),
            V((2, 8, D), F32),
            V((4, 8, D), F32),
            V((4, 8, D), F32),
            V((4, 8, D), F32),
            V((2, 8, D), F32),
            V((4, 8, 128), F32),
            V((4, 8, 128), F32),
            V((4, 8, 128), F32),
            V((2, 8, 128), F32),
            V((8, D), F32),
            V((16, D), F32),
            V((8, D), F32),
            V(rows, F32),
            V(rows, low),
            V((SEQS, LEN, LEN), F32),
            V((2, ROWS, D), low),
            V((4, ROWS, 256), low),
            V((SEQS, 4, WIDE, LEN), low),
            V((4, ROWS, 256), low),
            V(rows, F32),
            V(rows, low),
            V(rows, low),
            V(rows, low),
            V(rows, F32),
            V(rows, F32),
            V((4, ROWS, 256), low),
            V((2, ROWS, D), low),
            V((4, ROWS, 256), low),
            V(rows, low),
            V(rows, low),
            pltpu.SemaphoreType.DMA((COPIES,)),
            pltpu.SemaphoreType.DMA((COPIES,)),
            pltpu.SemaphoreType.DMA((4,)),
            pltpu.SemaphoreType.REGULAR,
        ],
        compiler_params=pltpu.CompilerParams(
            collective_id=0, has_side_effects=True, vmem_limit_bytes=64 * 2**20
        ),
    )(tokens, time_emb, segs, cotangent, wq, wo, wu, wd, norm)


def adam(weight, gradient, moment, second, step_rate, decay_rate):
    moment = BETA_ONE * moment + (1.0 - BETA_ONE) * gradient
    second = BETA_TWO * second + (1.0 - BETA_TWO) * gradient * gradient
    moment_hat = moment / (1.0 - BETA_ONE**STEP)
    second_hat = second / (1.0 - BETA_TWO**STEP)
    weight = weight - step_rate * (
        moment_hat / (jnp.sqrt(second_hat) + ADAM_EPS) + decay_rate * weight
    )
    return (moment, second, weight)


def step_kernel(
    out_in, grad_in, shards, norm_sum, square_sum, wq, wo, wu, wd, norm,
    qm, qs, om, os, um, us, dm, ds, nm, ns,
    out, grad, total, qm_new, qs_new, q_new, om_new, os_new, o_new, um_new, us_new, u_new, dm_new, ds_new, d_new,
    nm_new, ns_new, n_new, norm_grad, sem,
):
    copies = [
        pltpu.make_async_copy(out_in, out, sem.at[0]),
        pltpu.make_async_copy(grad_in, grad, sem.at[1]),
    ]
    for copy in copies:
        copy.start()
    grad_norm = jnp.sqrt(square_sum[0:1, 0:1])
    total[...] = grad_norm
    factor = jnp.minimum(1.0, CLIP_AT / (grad_norm + 1e-06))

    def put(refs, at, value):
        for ref, new in zip(refs, value):
            ref[at] = new

    first, second = shards[0, 0], shards[1, 0]
    tail = lambda v: jnp.concatenate([v[:, 256:], v[:, 192:256]], axis=1)
    for c, g in enumerate((first[:, :192], tail(first), second[:, :192])):
        put((qm_new, qs_new, q_new), c, adam(wq[c], g * factor, qm[c], qs[c], RATE_MATRIX, WEIGHT_DECAY))
    put((om_new, os_new, o_new), ..., adam(wo[...], tail(second) * factor, om[...], os[...], RATE_OUT, WEIGHT_DECAY))
    for half in range(2):
        at = (slice(None), pl.ds(WIDE * half, WIDE))
        g = shards[0, 1 + half] * factor
        put((um_new, us_new, u_new), at, adam(wu[at], g, um[at], us[at], RATE_MATRIX, WEIGHT_DECAY))
        g = shards[1, 1 + half] * factor
        put((dm_new, ds_new, d_new), at, adam(wd[at], g, dm[at], ds[at], RATE_MATRIX, WEIGHT_DECAY))
    start = lax.axis_index("dp") * 24
    rolled = pltpu.roll(norm_sum[...], lax.rem(D - start, D), 1)
    g = rolled[0:4, 0:24] * factor
    norm_grad[...] = g
    put((nm_new, ns_new, n_new), ..., adam(norm[...], g, nm[...], ns[...], RATE_VECTOR, 0.0))
    for copy in copies:
        copy.wait()


def step(out_in, grad_in, shards, norm_sum, square_sum, weights, moments):
    anywhere = pl.BlockSpec(memory_space=pl.ANY)
    near = pl.BlockSpec(memory_space=pltpu.VMEM)
    like = lambda v: jax.ShapeDtypeStruct(v.shape, v.dtype)
    shapes = [like(out_in), like(grad_in), jax.ShapeDtypeStruct((1, 1), F32)]
    for w in weights:
        shapes += [like(w)] * 3
    shapes.append(like(weights[-1]))
    return pl.pallas_call(
        step_kernel,
        name="step",
        out_shape=shapes,
        in_specs=[anywhere] * 2 + [near] * (3 + len(weights) + len(moments)),
        out_specs=[anywhere] * 2 + [near] * (len(shapes) - 2),
        scratch_shapes=[pltpu.SemaphoreType.DMA((2,))],
        compiler_params=pltpu.CompilerParams(vmem_limit_bytes=32 * 2**20),
    )(out_in, grad_in, shards, norm_sum, square_sum, *weights, *moments)


def body(
    tokens, time_emb, segments, cotangent, w_qkv, w_out, w_up, w_down, norm_params,
    qkv_first, qkv_second, out_first, out_second, up_first, up_second, down_first, down_second, norm_first, norm_second,
):
    weights = (w_qkv, w_out.T, w_up, w_down.T, norm_params)
    sent = layer(tokens, time_emb, segments, cotangent, *weights)
    moments = (
        qkv_first, qkv_second, out_first.T, out_second.T, up_first, up_second, down_first.T, down_second.T,
        norm_first, norm_second,
    )
    new = list(step(*sent, weights, moments))
    new[2] = new[2].reshape(())
    for k in (6, 7, 8, 12, 13, 14):
        new[k] = new[k].T
    return tuple(new)


def solution(mesh):
    return jax.shard_map(
        body,
        mesh=mesh,
        in_specs=(
            P("dp", None),
            P("dp", None),
            P("dp", None),
            P("dp", None),
            P(None, "dp", "mp"),
            P("mp", "dp"),
            P("dp", "mp"),
            P("mp", "dp"),
            P(None, "dp"),
            P(None, "dp", "mp"),
            P(None, "dp", "mp"),
            P("mp", "dp"),
            P("mp", "dp"),
            P("dp", "mp"),
            P("dp", "mp"),
            P("mp", "dp"),
            P("mp", "dp"),
            P(None, "dp"),
            P(None, "dp"),
        ),
        out_specs=(
            P("dp", None),
            P("dp", None),
            P(),
            P(None, "dp", "mp"),
            P(None, "dp", "mp"),
            P(None, "dp", "mp"),
            P("mp", "dp"),
            P("mp", "dp"),
            P("mp", "dp"),
            P("dp", "mp"),
            P("dp", "mp"),
            P("dp", "mp"),
            P("mp", "dp"),
            P("mp", "dp"),
            P("mp", "dp"),
            P(None, "dp"),
            P(None, "dp"),
            P(None, "dp"),
            P(None, "dp"),
        ),
        check_vma=False,
    )
```

time: 1220 us -> 173 us (0.14)
  waiting for transfers between devices: 740 us -> 0 us
  blocking collectives: 264 us -> 0 us
  Pallas kernels: 0 us -> 153 us
  matrix products: 92.8 us -> 0 us
  other arithmetic: 58.7 us -> 0 us
  between operations: 23.5 us -> 0.89 us
  local copies, waits for them, and re-layouts: 35.5 us -> 18.3 us
    psum x3 -> x0, waiting for transfers between devices: 355 us -> none  [the longest x1 127 us: micro_pass(): lax.psum(mlp_part.astype(jnp.bfloat16), 'mp').astype(jnp.float32)]
    reduce_scatter x6 -> x0, waiting for transfers between devices: 273 us -> none  [the longest x2 153 us: body(): lax.psum_scatter(grads_local[1].astype(jnp.bfloat16), 'dp', scatter_dimen...]
    pallas_call x0 -> x2, Pallas kernels: none -> 153 us  [the longest x1 149 us: layer(): pl.pallas_call(layer_kernel, name='layer', out_shape=(jax.ShapeDtypeStruc...]
    unnamed x1 -> x0, blocking collectives: 123 us -> none
    unnamed x13 -> x0, waiting for transfers between devices: 113 us -> none
    dot_general x36 -> x0, matrix products: 92.8 us -> none  [the longest x6 21.8 us: left_product(): lax.dot_general(first_arr, second_arr, (((0,), (0,)), ((), ())), preferre...]
    all_gather x3 -> x0, blocking collectives: 73.2 us -> none  [the longest x1 25.8 us: body(): lax.all_gather(norm_low, 'dp', axis=1, tiled=True)]
    psum x1 -> x0, blocking collectives: 67.5 us -> none  [body(): grad_norm = jnp.sqrt(lax.psum(squares, ('dp', 'mp')))]
  transfers between devices with their start and end apart: 12 -> 0, of which waited for: 8 -> 0; matrix products, arithmetic and copies ran while one was open for 10% -> 0% of each run, Pallas kernels for 0% -> 0%
where the time goes in v2:
time: 173 us; the launch traced here: 172 us
  Pallas kernels  153 us (88%)
  local copies, waits for them, and re-layouts  18.3 us (11%)
    pallas_call x1, Pallas kernels, layer(): pl.pallas_call(layer_kernel, name='layer', out_shape=(jax.ShapeDtypeStruc...  149 us
    unnamed x40, local copies, waits for them, and re-layouts  18.3 us
    pallas_call x1, Pallas kernels, step(): pl.pallas_call(step_kernel, name='step', out_shape=shapes, in_specs=[anyw...  3.6 us

profile of v2, /device:TPU:1, one launch (start us, length us, event | category | flops | bytes accessed | tf_op | source)
XLA Modules:
  0.0 171.8 jit_solution(6010827397718211134)
XLA Ops:
  0.7 149.0 %layer.1 = (bf16[2048,768]{1,0:T(8,128)(2,1)}, bf16[2048,768]{1,0:T(8,128)(2,1)}, f32[2,3,24,384]{3,2,1,0:T(8,128)}, f32[8,768]{1,0:T(8,128)}, f32[8,128]{1,0:T(8,128)}) custom-call(bf16[2048,768]{1,0:T(8,128)(2,1)} %tokens.1, bf16[16,768]{1,0:T(8,128)(2,1)} %time_emb.1, s32[16,128]{1,0:T(8,128)} %segs.1, bf16[2048,768]{1,0:T(8,128)(2,1)} %cotangent.1, ...), custom_call_target="tpu_custom_call" | custom-call | tf_op jit(solution)/shard_map/layer/pallas_call | solution.py:755
  149.6 0.0 copy-start
  149.6 1.9 %copy-done = bf16[2048,768]{1,0:T(8,128)(2,1)S(1)} copy-done((bf16[2048,768]{1,0:T(8,128)(2,1)S(1)}, bf16[2048,768]{1,0:T(8,128)(2,1)}, u32[]{:S(2)}) %copy-start) | copy-done | bytes 3145752
  151.5 0.0 copy-start.1
  151.5 1.9 %copy-done.1 = bf16[2048,768]{1,0:T(8,128)(2,1)S(1)} copy-done((bf16[2048,768]{1,0:T(8,128)(2,1)S(1)}, bf16[2048,768]{1,0:T(8,128)(2,1)}, u32[]{:S(2)}) %copy-start.1) | copy-done | bytes 3145752
  153.4 0.9 copy-done.2
  154.3 0.9 copy-done.3
  155.2 0.9 copy-done.4
  156.1 0.9 copy-done.5
  157.0 0.7 copy-done.6
  157.7 0.9 copy-done.7
  158.6 0.9 copy-done.8
  159.5 0.9 copy-done.9
  160.4 0.9 copy-done.10
  161.3 0.9 copy-done.11
  162.2 0.9 copy-done.12
  163.0 0.7 copy-done.13
  163.8 0.7 copy-done.14
  164.5 0.7 copy-done.15
  165.3 0.7 copy-done.16
  165.9 0.7 copy-done.17
  166.6 0.7 copy-done.18
  167.3 0.7 copy-done.19
  168.0 3.6 %step.1 = (bf16[2048,768]{1,0:T(8,128)(2,1)}, bf16[2048,768]{1,0:T(8,128)(2,1)}, f32[1,1]{1,0:T(1,128)}, f32[3,24,192]{2,1,0:T(8,128)}, f32[3,24,192]{2,1,0:T(8,...) custom-call(bf16[2048,768]{1,0:T(8,128)(2,1)S(1)} %copy-done, ...), custom_call_target="tpu_custom_call" | custom-call | tf_op jit(solution)/shard_map/step/pallas_call | solution.py:880
  (18 shorter events, 0.0 us)
Async XLA Ops:
  149.6 1.9 %copy-start = (bf16[2048,768]{1,0:T(8,128)(2,1)S(1)}, bf16[2048,768]{1,0:T(8,128)(2,1)}, u32[]{:S(2)}) copy-start(bf16[2048,768]{1,0:T(8,128)(2,1)} %get-tuple-element.43.out_in) | copy-start | bytes 9437188
  151.5 1.9 %copy-start.1 = (bf16[2048,768]{1,0:T(8,128)(2,1)S(1)}, bf16[2048,768]{1,0:T(8,128)(2,1)}, u32[]{:S(2)}) copy-start(bf16[2048,768]{1,0:T(8,128)(2,1)} %get-tuple-element.44.grad_in) | copy-start | bytes 9437188
  153.4 0.9 copy-start.2
  154.3 0.9 copy-start.3
  155.2 0.9 copy-start.4
  156.1 0.9 copy-start.5
  157.0 0.7 copy-start.6
  157.7 0.9 copy-start.7
  158.6 0.9 copy-start.8
  159.5 0.9 copy-start.9
  160.4 0.9 copy-start.10
  161.3 0.9 copy-start.11
  162.2 0.9 copy-start.12
  163.0 0.7 copy-start.13
  163.8 0.7 copy-start.14
  164.5 0.7 copy-start.15
  165.3 0.7 copy-start.16
  165.9 0.7 copy-start.17
  166.6 0.7 copy-start.18
  167.3 0.7 copy-start.19
